TPU v7x, 32 devices: a whole 2x2x4 slice. The times are simulated.
32 devices in a mesh: grid: 8 (over z, y), sub: 4 (over x, core).
Axes of the slice: x: 2, y: 2, z: 4, core: 2. Of those that a mesh axis runs over, the one named last changes fastest.
Arguments:
- field: float32 [5, 256, 32, 128], P(None, ('grid', 'sub')), may hold values from -6 to 6
- node_jitter: float32 [3, 256, 32, 128], P(None, ('grid', 'sub')), may hold values from -0.15 to 0.15
- time_ratio: float32 [256, 32, 128], P(('grid', 'sub')), may hold values from 0.2 to 5
- donor_cell: int32 [32, 8, 2, 128], P(('grid', 'sub')), may hold values from 0 to 32638, as said below
- receptor_offset: float32 [32, 8, 2, 3, 128], P(('grid', 'sub')), may hold values from 0.1 to 0.9
- receptor_node: int32 [32, 8, 2, 128], P(('grid', 'sub')), may hold values from 4096 to 28671, as said below
- point_count: int32 [32, 8], P(('grid', 'sub')), may hold values from 1 to 256, as said below
Outputs:
- relaxed: float32 [5, 256, 32, 128], P(None, ('grid', 'sub'))
Inputs may be any that keep to these rules, and one draw needn't show every extreme that they name: `donor_cell`: a cell i * 32 * 128 + j * 128 + k with i < 8, j < 31, k < 127. `receptor_node`: distinct over all slots of one source block, on local planes 1 to 6. `point_count`: from every block of grid g, owner (g + 1) mod 8 receives exactly 256 points, owner (g + 2) mod 8 receives one point, and every other owner at most 128.
All inputs are finite; a program needn't handle non-finite values.
Results may differ from a plain program's by a relative error of at most 0.0003.
Values sent between devices are 32-bit elements; how exact they have to be, the bound alone decides.
No kernel may reach another device: no remote copies, remote signals or barrier semaphores. Data moves between devices by JAX's collectives and lax.ppermute only.
A program may use at most 128 MiB of HBM per device.

v0:
```python
import functools

import jax
import jax.numpy as jnp
from jax import lax
from jax.experimental import pallas as pl
from jax.experimental.pallas import tpu as pltpu
from jax.sharding import PartitionSpec as P

ROWS = 8
LANES = 128
VMEM = pl.BlockSpec(memory_space=pltpu.VMEM)
HBM = pl.BlockSpec(memory_space=pltpu.HBM)
LIMIT = 24 << 20


def passed_along(value, axis, steps):
    count = lax.axis_size(axis)
    pairs = [(source, (source + steps) % count) for source in range(count)]
    return lax.ppermute(value, axis, pairs)


def first_kernel(
    count_ref, cell_ref, offset_ref, node_ref, field_ref, jitter_ref,
    message_ref, code_ref, next_ref, last_ref,
    count_smem, cell_vmem, offset_vmem, node_vmem, sem,
):
    owners, points = cell_ref.shape[1], cell_ref.shape[3]
    variables, planes, rows_count, _ = field_ref.shape
    copies = [
        pltpu.make_async_copy(source, target, sem.at[k])
        for k, (source, target) in enumerate(
            (
                (count_ref, count_smem),
                (cell_ref, cell_vmem),
                (offset_ref, offset_vmem),
                (node_ref, node_vmem),
                (jitter_ref.at[:, pl.ds(0, 1)], next_ref.at[pl.ds(0, 3)]),
                (field_ref.at[:, pl.ds(0, 1)], next_ref.at[pl.ds(3, variables)]),
                (field_ref.at[:, pl.ds(planes - 1, 1)], last_ref),
            )
        )
    ]
    for copy in copies:
        copy.start()
    for copy in copies[:4]:
        copy.wait()

    spare = (planes + 1) * rows_count * 8
    lane = lax.broadcasted_iota(jnp.int32, (1, points), 1)

    def coded(nodes, live):
        row = jnp.where(live, (nodes >> 7) * 8, spare)
        return row * LANES + (((nodes & 127) - lane) & 127)

    def one(owner, carry):
        count = count_smem[0, owner]
        more = count > points
        cells = cell_vmem[0, owner].astype(jnp.float32)
        counts = jnp.full((1, points), count, jnp.int32).astype(jnp.float32)
        message_ref[owner, 0:1, :] = cells[0:1]
        message_ref[owner, 4:5, :] = jnp.where(more, cells[1:2], counts)
        for c in range(3):
            message_ref[owner, 1 + c : 2 + c, :] = offset_vmem[0, owner, c, 0:1, :]
            message_ref[owner, 5 + c : 6 + c, :] = offset_vmem[0, owner, c, 1:2, :]
        nodes = node_vmem[0, owner]
        code_ref[pl.ds(owner, 1), :] = coded(nodes[0:1], lane < count)

        @pl.when(more)
        def _():
            code_ref[owners : owners + 1, :] = coded(nodes[1:2], lane + points < count)

        return carry

    lax.fori_loop(0, owners, one, 0, unroll=True)
    for copy in copies[4:]:
        copy.wait()


def coefficients(corner):
    linear = [corner[4] - corner[0], corner[2] - corner[0], corner[1] - corner[0]]
    pair_01 = corner[6] - corner[4] - linear[1]
    pair_02 = corner[5] - corner[4] - linear[2]
    pair_12 = corner[3] - corner[2] - linear[2]
    triple = (corner[7] - corner[6]) - (corner[5] - corner[4]) - pair_12
    return corner[0], linear, pair_01, pair_02, pair_12, triple


def solve(corner, target):
    polys = []
    for component in range(3):
        start, linear, pair_01, pair_02, pair_12, triple = coefficients(
            [corner(q, component) for q in range(8)]
        )
        linear[component] = linear[component] + 1.0
        polys.append((start - target[component], linear, pair_01, pair_02, pair_12, triple))
    s0 = s1 = s2 = jnp.full(target[0].shape, 0.5, jnp.float32)
    for _ in range(4):
        s01, s02, s12 = s0 * s1, s0 * s2, s1 * s2
        misfit, jac = [], []
        for start, (l0, l1, l2), p01, p02, p12, triple in polys:
            d0 = l0 + s1 * p01 + s2 * p02 + s12 * triple
            d1 = l1 + s0 * p01 + s2 * p12 + s02 * triple
            d2 = l2 + s0 * p02 + s1 * p12 + s01 * triple
            misfit.append(start + s0 * d0 + s1 * (l1 + s2 * p12) + s2 * l2)
            jac.append((d0, d1, d2))
        (a0, a1, a2), (b0, b1, b2), (c0, c1, c2) = jac
        m0, m1, m2 = misfit
        bc12 = b1 * c2 - b2 * c1
        bc02 = b0 * c2 - b2 * c0
        bc01 = b0 * c1 - b1 * c0
        det = a0 * bc12 - a1 * bc02 + a2 * bc01
        bm2 = m1 * c2 - b2 * m2
        bm1 = m1 * c1 - b1 * m2
        bm0 = b0 * m2 - m1 * c0
        inverse = 1.0 / det
        u0 = m0 * bc12 - a1 * bm2 + a2 * bm1
        u1 = a0 * bm2 - m0 * bc02 + a2 * bm0
        u2 = a0 * (b1 * m2 - m1 * c1) - a1 * bm0 + m0 * bc01
        s0 = s0 - u0 * inverse
        s1 = s1 - u1 * inverse
        s2 = s2 - u2 * inverse
    values = []
    for variable in range(5):
        u = [corner(q, 3 + variable) for q in range(8)]
        e = [u[q] + s2 * (u[q + 1] - u[q]) for q in (0, 2, 4, 6)]
        f = [e[q] + s1 * (e[q + 1] - e[q]) for q in (0, 2)]
        values.append(f[0] + s0 * (f[1] - f[0]))
    return values


def table_kernel(field_ref, jitter_ref, next_ref, table_ref):
    planes, rows_count, columns = field_ref.shape[1:]

    def one_plane(plane, read):
        for half in range(2):
            tile = jnp.concatenate([read(4 * half + w) for w in range(4)], 0).T
            first = plane * (2 * columns) + half
            table_ref[pl.ds(first, columns, stride=2), :] = tile

    for plane in range(planes):
        one_plane(
            plane, lambda v: jitter_ref[v, plane] if v < 3 else field_ref[v - 3, plane]
        )
    one_plane(planes, lambda v: next_ref[v, 0])


def separated(tiles, lane):
    for bit, distance in ((0, 1), (1, 32), (2, 64)):
        low = (lane & distance) == 0
        result = list(tiles)
        for a in range(8):
            b = a | (1 << bit)
            if a == b:
                continue
            result[a] = jnp.where(low, tiles[a], pltpu.roll(tiles[b], distance, 1))
            result[b] = jnp.where(low, pltpu.roll(tiles[a], LANES - distance, 1), tiles[b])
        tiles = result
    return tiles


def tile_rows(tile):
    first = tile * ROWS
    return pl.ds(first if isinstance(first, int) else pl.multiple_of(first, ROWS), ROWS)


def each_source(owners, body):
    if owners <= 8:
        for source in range(owners + 1):
            body(source, 0)
    else:
        lax.fori_loop(0, owners + 1, body, 0)


def gather_kernel(owners, table_ref, message_ref, out_ref, decoded, codes, picked, parts, sem):
    rows_count = 32
    me = lax.axis_index("grid")
    heavy = lax.rem(me + owners - 1, owners)
    lane = lax.broadcasted_iota(jnp.int32, (ROWS, LANES), 1)
    sublane = lax.broadcasted_iota(jnp.int32, (ROWS, LANES), 0)

    def decode(cells, place):
        cells = cells.astype(jnp.int32)
        row = (cells >> 12) * (2 * LANES) + (cells & 127) * 2
        shift = ((lane & 30) - ((cells >> 7) & (rows_count - 1))) & 127
        decoded[place, :] = row * LANES + shift

    for block in range(owners // ROWS):
        cells = message_ref[pl.ds(block * ROWS * 8, ROWS, stride=8), :]
        decode(cells, pl.ds(block * ROWS, ROWS))
    more = jnp.broadcast_to(message_ref[pl.ds(heavy * 8 + 4, 1), :], (ROWS, LANES))
    decode(more, pl.ds(owners, ROWS))
    copy = pltpu.make_async_copy(decoded, codes, sem)
    copy.start()
    copy.wait()

    low = sublane < 4
    pairs = [(lane & 30) == 2 * k for k in range(16)]

    def one_source(source, carry):
        for block in range(4):
            held = [None, None]
            for k in range(32):
                code = codes[source, block * 32 + k]
                row = code >> 7
                tile = jnp.where(
                    low,
                    table_ref[pl.ds(row, ROWS), :],
                    table_ref[pl.ds(row + (2 * LANES - 4), ROWS), :],
                )
                tile = pltpu.roll(tile, code & 127, 1)
                k2 = k & 1
                held[k2] = tile if held[k2] is None else jnp.where(pairs[k >> 1], tile, held[k2])
            for k in range(2):
                picked[tile_rows((2 * block + k) * (owners + 1) + source), :] = held[k]
        return carry

    each_source(owners, one_source)

    def one_block(block, last):
        for s in range(8):
            tiles = [
                picked[pl.ds((g * (owners + 1) + block * ROWS) * 8 + s, ROWS, stride=8), :]
                for g in range(8)
            ]
            for x, tile in enumerate(separated(tiles, lane)):
                parts[s, x] = tile
        if last:
            tiles = [picked[pl.ds((g * (owners + 1) + owners) * 8, 8), :] for g in range(8)]
            for x, tile in enumerate(separated(tiles, lane)):
                parts[8, x] = tile

        def corner(q, variable):
            a0, a1, a2 = q >> 2, (q >> 1) & 1, q & 1
            s, x = 4 * a0 + 2 * a2 + (variable >> 2), 2 * (variable & 3) + a1
            tile = parts[s, x]
            if last:
                more = jnp.broadcast_to(parts[8, x, s : s + 1, :], (ROWS, LANES))
                tile = jnp.concatenate([tile, more], 0)
            return tile

        target = []
        for c in range(3):
            tile = message_ref[pl.ds(block * (ROWS * 8) + 1 + c, ROWS, stride=8), :]
            if last:
                more = message_ref[pl.ds(heavy * 8 + 5 + c, 1), :]
                tile = jnp.concatenate([tile, jnp.broadcast_to(more, (ROWS, LANES))], 0)
            target.append(tile)
        values = solve(corner, target)
        for variable in range(5):
            place = pl.ds(block * (ROWS * 16) + variable, ROWS, stride=16)
            out_ref[place, :] = values[variable][:ROWS]
            if last:
                out_ref[pl.ds(heavy * 16 + 8 + variable, 1), :] = values[variable][ROWS : ROWS + 1]

    for block in range(owners // ROWS):
        one_block(block, block == owners // ROWS - 1)


def relax_kernel(
    owners, code_ref, field_ref, below_ref, above_ref, ratio_ref, values_ref, out_ref,
    table, codes, out_vmem, sem, out_sem,
):
    variables, planes, rows_count, _ = field_ref.shape
    width = 8
    blocks = rows_count // ROWS
    plane_rows = rows_count * width

    copy = pltpu.make_async_copy(code_ref, codes, sem)
    copy.start()

    def put(plane, block, variable, tile):
        first = plane * plane_rows + block * ROWS * width + variable
        table[pl.ds(first, ROWS, stride=width), :] = tile

    zero = jnp.zeros((ROWS, LANES), jnp.float32)
    for block in range(blocks):
        place = pl.ds(block * ROWS, ROWS)
        for variable in range(variables):
            put(0, block, variable, below_ref[variable, 0, place, :])
            put(planes + 1, block, variable, above_ref[3 + variable, 0, place, :])
            for plane in range(planes):
                put(plane + 1, block, variable, field_ref[variable, plane, place, :])
        for plane in range(planes):
            put(plane + 1, block, variables, zero)

    copy.wait()
    lane = lax.broadcasted_iota(jnp.int32, (ROWS, LANES), 1)
    sublane = lax.broadcasted_iota(jnp.int32, (ROWS, LANES), 0)

    heavy = lax.rem(lax.axis_index("grid") + 1, owners)

    def one_source(source, carry):
        if isinstance(source, int):
            first = 16 * source if source < owners else heavy * 16 + 8
        else:
            more = source == owners
            first = jnp.where(more, heavy * 16 + 8, source * 16)
        if not isinstance(first, int):
            first = pl.multiple_of(first, 8)
        tile = jnp.where(sublane == variables, 1.0, values_ref[pl.ds(first, 8), :])
        for point in range(LANES):
            code = codes[source, point]
            shift = code & 127
            row = pl.multiple_of((code >> 7) + plane_rows, width)
            pltpu.store(
                table.at[pl.ds(row, width), :],
                pltpu.roll(tile, shift, 1),
                mask=((lane - point) & 127) == shift,
            )
        return carry

    each_source(owners, one_source)

    def out_copy(plane):
        return pltpu.make_async_copy(
            out_vmem.at[:, pl.ds(plane, 1)], out_ref.at[:, pl.ds(plane, 1)], out_sem.at[plane]
        )

    def one_plane(plane):
        for block in range(blocks):
            ratio = ratio_ref[plane, pl.ds(block * ROWS, ROWS), :]
            inverse = 1.0 / (1.0 + 6.0 * ratio)
            base = (plane + 1) * plane_rows + block * ROWS * width

            def get(step, variable):
                return table[pl.ds(base + step * width + variable, ROWS, stride=width), :]

            fringe = get(0, variables) > 0.5
            for variable in range(variables):
                here = get(0, variable)
                up, down = get(1, variable), get(-1, variable)
                if block == 0:
                    down = jnp.where(sublane == 0, 0.0, down)
                if block == blocks - 1:
                    up = jnp.where(sublane == ROWS - 1, 0.0, up)
                right = jnp.where(lane == LANES - 1, 0.0, pltpu.roll(here, LANES - 1, 1))
                left = jnp.where(lane == 0, 0.0, pltpu.roll(here, 1, 1))
                total = get(rows_count, variable) + get(-rows_count, variable)
                total = total + up + down + right + left
                smooth = (here + ratio * total) * inverse
                out_vmem[variable, plane, pl.ds(block * ROWS, ROWS), :] = jnp.where(
                    fringe, here, smooth
                )
        out_copy(plane).start()

    for plane in range(planes):
        one_plane(plane)
    for plane in range(planes):
        out_copy(plane).wait()


def on_device(
    field, node_jitter, time_ratio, donor_cell, receptor_offset, receptor_node, point_count
):
    variables, planes, rows_count, cols_count = field.shape
    owners, points = donor_cell.shape[1], donor_cell.shape[3]
    params = pltpu.CompilerParams(vmem_limit_bytes=LIMIT)
    offsets = jnp.swapaxes(receptor_offset, 2, 3)
    f32, i32 = jnp.float32, jnp.int32
    message, codes, first, last = pl.pallas_call(
        first_kernel,
        out_shape=[
            jax.ShapeDtypeStruct((owners, 8, LANES), f32),
            jax.ShapeDtypeStruct((owners + 8, LANES), i32),
            jax.ShapeDtypeStruct((3 + variables, 1, rows_count, cols_count), f32),
            jax.ShapeDtypeStruct((variables, 1, rows_count, cols_count), f32),
        ],
        in_specs=[HBM] * 6,
        out_specs=[VMEM] * 4,
        scratch_shapes=[
            pltpu.SMEM(point_count.shape, i32),
            pltpu.VMEM(donor_cell.shape, i32),
            pltpu.VMEM(offsets.shape, f32),
            pltpu.VMEM(receptor_node.shape, i32),
            pltpu.SemaphoreType.DMA((7,)),
        ],
        compiler_params=params,
        name="first",
    )(*[
        pltpu.with_memory_space_constraint(x, pltpu.HBM)
        for x in (point_count, donor_cell, offsets, receptor_node, field, node_jitter)
    ])
    following = passed_along(first, "sub", -1)
    below = passed_along(last, "sub", 1)
    message = lax.all_to_all(message, "grid", split_axis=0, concat_axis=0, tiled=True)
    table = pl.pallas_call(
        table_kernel,
        out_shape=jax.ShapeDtypeStruct(((planes + 1) * cols_count * 2, LANES), f32),
        in_specs=[VMEM] * 3,
        out_specs=VMEM,
        compiler_params=params,
        cost_estimate=pl.CostEstimate(flops=0, bytes_accessed=8 << 20, transcendentals=0),
        name="table",
    )(field, node_jitter, following)
    values = pl.pallas_call(
        functools.partial(gather_kernel, owners),
        out_shape=jax.ShapeDtypeStruct((owners * 16, LANES), f32),
        in_specs=[VMEM, VMEM],
        out_specs=VMEM,
        scratch_shapes=[
            pltpu.VMEM((owners + 8, LANES), i32),
            pltpu.SMEM((owners + 8, LANES), i32),
            pltpu.VMEM((8 * (owners + 1) * 8, LANES), f32),
            pltpu.VMEM((9, 8, ROWS, LANES), f32),
            pltpu.SemaphoreType.DMA,
        ],
        compiler_params=params,
        name="gather",
    )(table, message.reshape(owners * 8, LANES))
    values = values.reshape(owners, 16, LANES)
    values = lax.all_to_all(values, "grid", split_axis=0, concat_axis=0, tiled=True)
    return pl.pallas_call(
        functools.partial(relax_kernel, owners),
        out_shape=jax.ShapeDtypeStruct(field.shape, f32),
        in_specs=[VMEM] * 6,
        out_specs=HBM,
        scratch_shapes=[
            pltpu.VMEM(((planes + 2) * rows_count * 8 + 8, LANES), f32),
            pltpu.SMEM((owners + 8, LANES), i32),
            pltpu.VMEM(field.shape, f32),
            pltpu.SemaphoreType.DMA,
            pltpu.SemaphoreType.DMA((planes,)),
        ],
        compiler_params=params,
        name="relax",
    )(
        codes, field, below, following, time_ratio,
        values.reshape(owners * 16, LANES),
    )


def solution(mesh):
    placed = (
        P(None, ("grid", "sub"), None, None),
        P(None, ("grid", "sub"), None, None),
        P(("grid", "sub"), None, None),
        P(("grid", "sub"), None, None, None),
        P(("grid", "sub"), None, None, None, None),
        P(("grid", "sub"), None, None, None),
        P(("grid", "sub"), None),
    )
    return jax.shard_map(
        on_device,
        mesh=mesh,
        in_specs=placed,
        out_specs=P(None, ("grid", "sub"), None, None),
        check_vma=False,
    )
```

profile of v0, /device:TPU:0, one launch (start us, length us, event | category | flops | bytes accessed | tf_op | source)
XLA Modules:
  0.0 34.2 jit_solution(10237541596170978669)
XLA Ops:
  0.0 0.0 copy-start
  0.0 0.0 copy-start.1
  0.0 1.8 %first.1 = (f32[8,8,128]{2,1,0:T(8,128)}, s32[16,128]{1,0:T(8,128)S(1)}, f32[8,1,32,128]{3,2,1,0:T(8,128)S(1)}, f32[5,1,32,128]{3,2,1,0:T(8,128)S(1)}) custom-call(s32[1,8]{1,0:T(1,128)} %count_ref.1, s32[1,8,2,128]{3,2,1,0:T(2,128)} %cell_ref.1, f32[1,8,3,2,128]{4,3,2,1,0:T(2,128)} %bitcast.6, s32[1,8,2,128]{3,2,1,0:T(2,128)} %node_ref.1, ...), custom_call_target="tpu_custom_call" | custom-call | tf_op jit(solution)/shard_map/first/pallas_call | solution.py:361
  1.8 2.4 %collective-permute-start.1 = (f32[8,1,32,128]{3,2,1,0:T(8,128)S(1)}, f32[8,1,32,128]{3,2,1,0:T(8,128)S(1)}, u32[]{:S(2)}, u32[]{:S(2)}) collective-permute-start(f32[8,1,32,128]{3,2,1,0:T(8,128)S(1)} %get-tuple-element.11), channel_id=1, source_target_pairs={{0,3},{1,0},{2,1},{3,2},{4,7},{5,4},{6,5},{7,6},{8,11},{9,8},{10,9... | collective-permute-start | bytes 393224 | tf_op jit(solution)/shard_map/ppermute | solution.py:20
  4.2 5.8 %all-to-all-start = ((f32[8,8,128]{2,1,0:T(8,128)}), f32[8,8,128]{2,1,0:T(8,128)S(1)}, u32[]{:S(2)}, u32[]{:S(2)}) async-start(f32[8,8,128]{2,1,0:T(8,128)} %get-tuple-element.12), calls=%async_computation | async-start | bytes 65536 | tf_op jit(solution)/shard_map/all_to_all | solution.py:386
  10.0 0.0 collective-permute-done.1.next_ref.above_ref
  10.0 0.0 copy-done
  10.1 0.0 copy-done.1
  10.1 0.4 %table.1.table_ref = f32[2304,128]{1,0:T(8,128)S(1)} custom-call(f32[5,8,32,128]{3,2,1,0:T(8,128)S(1)} %copy-done, f32[3,8,32,128]{3,2,1,0:T(8,128)S(1)} %copy-done.1, f32[8,1,32,128]{3,2,1,0:T(8,128)S(1)} %collective-permute-done.1.next_ref.above_ref), custom_call_target="tpu_custom_call" | custom-call | bytes 8388608 | tf_op jit(solution)/shard_map/table/pallas_call | solution.py:387
  10.4 0.0 copy-start.2
  10.5 6.3 %all-to-all-done = f32[8,8,128]{2,1,0:T(8,128)S(1)} async-done(((f32[8,8,128]{2,1,0:T(8,128)}), f32[8,8,128]{2,1,0:T(8,128)S(1)}, u32[]{:S(2)}, u32[]{:S(2)}) %all-to-all-start) | async-done | bytes 32800 | tf_op jit(solution)/shard_map/all_to_all | solution.py:386
  16.7 3.2 %gather.1 = f32[128,128]{1,0:T(8,128)} custom-call(f32[2304,128]{1,0:T(8,128)S(1)} %table.1.table_ref, f32[64,128]{1,0:T(8,128)S(1)} %bitcast.5), custom_call_target="tpu_custom_call" | custom-call | tf_op jit(solution)/shard_map/gather/pallas_call | solution.py:396
  19.9 3.4 %all-to-all-start.1 = ((f32[8,16,128]{2,1,0:T(8,128)}), f32[8,16,128]{2,1,0:T(8,128)S(1)}, u32[]{:S(2)}, u32[]{:S(2)}) async-start(f32[8,16,128]{2,1,0:T(8,128)} %bitcast.2), calls=%async_computation.1 | async-start | bytes 131072 | tf_op jit(solution)/shard_map/all_to_all | solution.py:412
  23.3 0.1 collective-permute-start
  23.3 3.9 %collective-permute-done.below_ref = f32[5,1,32,128]{3,2,1,0:T(8,128)S(1)} collective-permute-done((f32[5,1,32,128]{3,2,1,0:T(8,128)S(1)}, f32[5,1,32,128]{3,2,1,0:T(8,128)S(1)}, u32[]{:S(2)}, u32[]{:S(2)}) %collective-permute-start) | collective-permute-done | bytes 81952 | tf_op jit(solution)/shard_map/ppermute | solution.py:20
  27.2 2.9 %all-to-all-done.1 = f32[8,16,128]{2,1,0:T(8,128)S(1)} async-done(((f32[8,16,128]{2,1,0:T(8,128)}), f32[8,16,128]{2,1,0:T(8,128)S(1)}, u32[]{:S(2)}, u32[]{:S(2)}) %all-to-all-start.1) | async-done | bytes 65568 | tf_op jit(solution)/shard_map/all_to_all | solution.py:412
  30.1 0.0 copy-done.2
  30.1 4.0 %relax.1 = f32[5,8,32,128]{3,2,1,0:T(8,128)} custom-call(s32[16,128]{1,0:T(8,128)S(1)} %get-tuple-element.9.code_ref, f32[5,8,32,128]{3,2,1,0:T(8,128)S(1)} %copy-done, f32[5,1,32,128]{3,2,1,0:T(8,128)S(1)} %collective-permute-done.below_ref, f32[8,1,32,128]{3,2,1,0:T(8,128)S(1)} %collective-permute-done.1.next_ref.above_ref, f32[8,32,128]{2,1,0:T(8,128)S(1)} %copy-done.2, ...), custom_call_target="tpu_custom_call" | custom-call | tf_op jit(solution)/shard_map/relax/pallas_call | solution.py:413
Async XLA Ops:
  0.0 10.0 %copy-start = (f32[5,8,32,128]{3,2,1,0:T(8,128)S(1)}, f32[5,8,32,128]{3,2,1,0:T(8,128)}, u32[]{:S(2)}) copy-start(f32[5,8,32,128]{3,2,1,0:T(8,128)} %field_ref.5) | copy-start | bytes 1966084
  0.0 10.1 %copy-start.1 = (f32[3,8,32,128]{3,2,1,0:T(8,128)S(1)}, f32[3,8,32,128]{3,2,1,0:T(8,128)}, u32[]{:S(2)}) copy-start(f32[3,8,32,128]{3,2,1,0:T(8,128)} %jitter_ref.3) | copy-start | bytes 1179652
  1.8 8.3 %collective-permute-start.1 = (f32[8,1,32,128]{3,2,1,0:T(8,128)S(1)}, f32[8,1,32,128]{3,2,1,0:T(8,128)S(1)}, u32[]{:S(2)}, u32[]{:S(2)}) collective-permute-start(f32[8,1,32,128]{3,2,1,0:T(8,128)S(1)} %get-tuple-element.11), channel_id=1, source_target_pairs={{0,3},{1,0},{2,1},{3,2},{4,7},{5,4},{6,5},{7,6},{8,11},{9,8},{10,9... | collective-permute-start | bytes 393224 | tf_op jit(solution)/shard_map/ppermute | solution.py:20
  4.2 12.5 %all-to-all-start = ((f32[8,8,128]{2,1,0:T(8,128)}), f32[8,8,128]{2,1,0:T(8,128)S(1)}, u32[]{:S(2)}, u32[]{:S(2)}) async-start(f32[8,8,128]{2,1,0:T(8,128)} %get-tuple-element.12), calls=%async_computation | async-start | bytes 65536 | tf_op jit(solution)/shard_map/all_to_all | solution.py:386
  10.4 19.7 %copy-start.2 = (f32[8,32,128]{2,1,0:T(8,128)S(1)}, f32[8,32,128]{2,1,0:T(8,128)}, u32[]{:S(2)}) copy-start(f32[8,32,128]{2,1,0:T(8,128)} %ratio_ref.1) | copy-start | bytes 393220
  19.9 10.2 %all-to-all-start.1 = ((f32[8,16,128]{2,1,0:T(8,128)}), f32[8,16,128]{2,1,0:T(8,128)S(1)}, u32[]{:S(2)}, u32[]{:S(2)}) async-start(f32[8,16,128]{2,1,0:T(8,128)} %bitcast.2), calls=%async_computation.1 | async-start | bytes 131072 | tf_op jit(solution)/shard_map/all_to_all | solution.py:412
  23.3 3.9 %collective-permute-start = (f32[5,1,32,128]{3,2,1,0:T(8,128)S(1)}, f32[5,1,32,128]{3,2,1,0:T(8,128)S(1)}, u32[]{:S(2)}, u32[]{:S(2)}) collective-permute-start(f32[5,1,32,128]{3,2,1,0:T(8,128)S(1)} %get-tuple-element.10), channel_id=1, source_target_pairs={{0,1},{1,2},{2,3},{3,0},{4,5},{5,6},{6,7},{7,4},{8,9},{9,10},{10,1... | collective-permute-start | bytes 245768 | tf_op jit(solution)/shard_map/ppermute | solution.py:20
where the time goes:
time: 34.5 us; the launch traced here: 34.2 us
  waiting for transfers between devices  13.1 us (38%)
  starting transfers between devices  11.7 us (34%)
  Pallas kernels  9.33 us (27%)
    all_to_all x1, waiting for transfers between devices, on_device(): lax.all_to_all(message, 'grid', split_axis=0, concat_axis=0, tiled=True)  6.27 us
    all_to_all x1, starting transfers between devices, on_device(): lax.all_to_all(message, 'grid', split_axis=0, concat_axis=0, tiled=True)  5.84 us
    pallas_call x1, Pallas kernels, on_device(): pl.pallas_call(functools.partial(relax_kernel, owners), out_shape=jax.Sha...  4.04 us
    ppermute x2, waiting for transfers between devices, passed_along(): return lax.ppermute(value, axis, pairs)  3.86 us
    all_to_all x1, starting transfers between devices, on_device(): lax.all_to_all(values, 'grid', split_axis=0, concat_axis=0, tiled=True)  3.36 us
    pallas_call x1, Pallas kernels, on_device(): pl.pallas_call(functools.partial(gather_kernel, owners), out_shape=jax.Sh...  3.16 us
    all_to_all x1, waiting for transfers between devices, on_device(): lax.all_to_all(values, 'grid', split_axis=0, concat_axis=0, tiled=True)  2.92 us
    ppermute x2, starting transfers between devices, passed_along(): return lax.ppermute(value, axis, pairs)  2.49 us
  transfers between devices with their start and end apart: 4, of which 3 were waited for; matrix products, arithmetic and copies ran while one was open for 0% of the time, Pallas kernels for 1%

commit v1 on v0

--- a/solution.py
+++ b/solution.py
@@ -49,9 +49,9 @@
     spare = (planes + 1) * rows_count * 8
     lane = lax.broadcasted_iota(jnp.int32, (1, points), 1)
 
-    def coded(nodes, live):
-        row = jnp.where(live, (nodes >> 7) * 8, spare)
-        return row * LANES + (((nodes & 127) - lane) & 127)
+    def code(place, nodes, live):
+        code_ref[0, place, :] = jnp.where(live, (nodes >> 7) * 8, spare)
+        code_ref[1, place, :] = ((nodes & 127) - lane) & 127
 
     def one(owner, carry):
         count = count_smem[0, owner]
@@ -64,11 +64,11 @@
             message_ref[owner, 1 + c : 2 + c, :] = offset_vmem[0, owner, c, 0:1, :]
             message_ref[owner, 5 + c : 6 + c, :] = offset_vmem[0, owner, c, 1:2, :]
         nodes = node_vmem[0, owner]
-        code_ref[pl.ds(owner, 1), :] = coded(nodes[0:1], lane < count)
+        code(pl.ds(owner, 1), nodes[0:1], lane < count)
 
         @pl.when(more)
         def _():
-            code_ref[owners : owners + 1, :] = coded(nodes[1:2], lane + points < count)
+            code(pl.ds(owners, 1), nodes[1:2], lane + points < count)
 
         return carry
 
@@ -129,8 +129,16 @@
     return values
 
 
-def table_kernel(field_ref, jitter_ref, next_ref, table_ref):
-    planes, rows_count, columns = field_ref.shape[1:]
+def table_kernel(
+    field_ref, jitter_ref, next_ref, below_ref, table_ref, rows_ref, field, jitter, sem
+):
+    variables, planes, rows_count, columns = field_ref.shape
+    copies = [
+        pltpu.make_async_copy(field_ref, field, sem.at[0]),
+        pltpu.make_async_copy(jitter_ref, jitter, sem.at[1]),
+    ]
+    for copy in copies:
+        copy.start()
 
     def one_plane(plane, read):
         for half in range(2):
@@ -138,11 +146,22 @@
             first = plane * (2 * columns) + half
             table_ref[pl.ds(first, columns, stride=2), :] = tile
 
+    def put(plane, variable, tile):
+        first = plane * rows_count * 8 + variable
+        rows_ref[pl.ds(first, rows_count, stride=8), :] = tile
+
+    one_plane(planes, lambda v: next_ref[v, 0])
+    for variable in range(variables):
+        put(0, variable, below_ref[variable, 0])
+        put(planes + 1, variable, next_ref[3 + variable, 0])
     for plane in range(planes):
-        one_plane(
-            plane, lambda v: jitter_ref[v, plane] if v < 3 else field_ref[v - 3, plane]
-        )
-    one_plane(planes, lambda v: next_ref[v, 0])
+        put(plane + 1, variables, jnp.zeros((rows_count, columns), jnp.float32))
+    for copy in copies:
+        copy.wait()
+    for plane in range(planes):
+        one_plane(plane, lambda v: jitter[v, plane] if v < 3 else field[v - 3, plane])
+        for variable in range(variables):
+            put(plane + 1, variable, field[variable, plane])
 
 
 def separated(tiles, lane):
@@ -258,59 +277,61 @@
 
 
 def relax_kernel(
-    owners, code_ref, field_ref, below_ref, above_ref, ratio_ref, values_ref, out_ref,
-    table, codes, out_vmem, sem, out_sem,
+    owners, rows_ref, code_ref, ratio_ref, values_ref, out_ref, table, codes, rolled, out_vmem,
+    sem, out_sem,
 ):
-    variables, planes, rows_count, _ = field_ref.shape
+    variables, planes, rows_count, _ = out_ref.shape
     width = 8
     blocks = rows_count // ROWS
     plane_rows = rows_count * width
-
     copy = pltpu.make_async_copy(code_ref, codes, sem)
     copy.start()
-
-    def put(plane, block, variable, tile):
-        first = plane * plane_rows + block * ROWS * width + variable
-        table[pl.ds(first, ROWS, stride=width), :] = tile
-
-    zero = jnp.zeros((ROWS, LANES), jnp.float32)
-    for block in range(blocks):
-        place = pl.ds(block * ROWS, ROWS)
-        for variable in range(variables):
-            put(0, block, variable, below_ref[variable, 0, place, :])
-            put(planes + 1, block, variable, above_ref[3 + variable, 0, place, :])
-            for plane in range(planes):
-                put(plane + 1, block, variable, field_ref[variable, plane, place, :])
-        for plane in range(planes):
-            put(plane + 1, block, variables, zero)
-
-    copy.wait()
     lane = lax.broadcasted_iota(jnp.int32, (ROWS, LANES), 1)
     sublane = lax.broadcasted_iota(jnp.int32, (ROWS, LANES), 0)
-
     heavy = lax.rem(lax.axis_index("grid") + 1, owners)
-
-    def one_source(source, carry):
+    for plane in range(planes + 2):
+        place = pl.ds(plane * plane_rows, plane_rows)
+        table[place, :] = rows_ref[place, :]
+    copy.wait()
+
+    def rotate(source, half):
         if isinstance(source, int):
             first = 16 * source if source < owners else heavy * 16 + 8
         else:
-            more = source == owners
-            first = jnp.where(more, heavy * 16 + 8, source * 16)
+            first = jnp.where(source == owners, heavy * 16 + 8, source * 16)
         if not isinstance(first, int):
             first = pl.multiple_of(first, 8)
         tile = jnp.where(sublane == variables, 1.0, values_ref[pl.ds(first, 8), :])
+        tile = jnp.where(sublane == variables + 1, lane.astype(jnp.float32), tile)
         for point in range(LANES):
-            code = codes[source, point]
-            shift = code & 127
-            row = pl.multiple_of((code >> 7) + plane_rows, width)
+            place = (half * LANES + point) * ROWS
+            rolled[place : place + ROWS, :] = pltpu.roll(tile, codes[1, source, point], 1)
+
+    def store(source, half):
+        for point in range(LANES):
+            place = (half * LANES + point) * ROWS
+            tag = rolled[place + variables + 1 : place + variables + 2, :]
+            row = pl.multiple_of(codes[0, source, point] + plane_rows, width)
             pltpu.store(
                 table.at[pl.ds(row, width), :],
-                pltpu.roll(tile, shift, 1),
-                mask=((lane - point) & 127) == shift,
+                rolled[place : place + ROWS, :],
+                mask=jnp.broadcast_to(tag, (ROWS, LANES)) == float(point),
             )
-        return carry
-
-    each_source(owners, one_source)
+
+    if owners <= 8:
+        rotate(0, 0)
+        for source in range(owners + 1):
+            if source < owners:
+                rotate(source + 1, (source + 1) % 2)
+            store(source, source % 2)
+    else:
+
+        def one_source(source, carry):
+            rotate(source, 0)
+            store(source, 0)
+            return carry
+
+        lax.fori_loop(0, owners + 1, one_source, 0)
 
     def out_copy(plane):
         return pltpu.make_async_copy(
@@ -357,12 +378,15 @@
     owners, points = donor_cell.shape[1], donor_cell.shape[3]
     params = pltpu.CompilerParams(vmem_limit_bytes=LIMIT)
     offsets = jnp.swapaxes(receptor_offset, 2, 3)
+    field, node_jitter = (
+        pltpu.with_memory_space_constraint(x, pltpu.HBM) for x in (field, node_jitter)
+    )
     f32, i32 = jnp.float32, jnp.int32
     message, codes, first, last = pl.pallas_call(
         first_kernel,
         out_shape=[
             jax.ShapeDtypeStruct((owners, 8, LANES), f32),
-            jax.ShapeDtypeStruct((owners + 8, LANES), i32),
+            jax.ShapeDtypeStruct((2, owners + 8, LANES), i32),
             jax.ShapeDtypeStruct((3 + variables, 1, rows_count, cols_count), f32),
             jax.ShapeDtypeStruct((variables, 1, rows_count, cols_count), f32),
         ],
@@ -379,20 +403,29 @@
         name="first",
     )(*[
         pltpu.with_memory_space_constraint(x, pltpu.HBM)
-        for x in (point_count, donor_cell, offsets, receptor_node, field, node_jitter)
-    ])
+        for x in (point_count, donor_cell, offsets, receptor_node)
+    ], field, node_jitter)
     following = passed_along(first, "sub", -1)
     below = passed_along(last, "sub", 1)
     message = lax.all_to_all(message, "grid", split_axis=0, concat_axis=0, tiled=True)
-    table = pl.pallas_call(
+    sweep_rows = (planes + 2) * rows_count * 8
+    table, rows = pl.pallas_call(
         table_kernel,
-        out_shape=jax.ShapeDtypeStruct(((planes + 1) * cols_count * 2, LANES), f32),
-        in_specs=[VMEM] * 3,
-        out_specs=VMEM,
+        out_shape=[
+            jax.ShapeDtypeStruct(((planes + 1) * cols_count * 2, LANES), f32),
+            jax.ShapeDtypeStruct((sweep_rows, LANES), f32),
+        ],
+        in_specs=[HBM, HBM, VMEM, VMEM],
+        out_specs=[VMEM, VMEM],
+        scratch_shapes=[
+            pltpu.VMEM(field.shape, f32),
+            pltpu.VMEM(node_jitter.shape, f32),
+            pltpu.SemaphoreType.DMA((2,)),
+        ],
         compiler_params=params,
         cost_estimate=pl.CostEstimate(flops=0, bytes_accessed=8 << 20, transcendentals=0),
         name="table",
-    )(field, node_jitter, following)
+    )(field, node_jitter, following, below)
     values = pl.pallas_call(
         functools.partial(gather_kernel, owners),
         out_shape=jax.ShapeDtypeStruct((owners * 16, LANES), f32),
@@ -413,21 +446,19 @@
     return pl.pallas_call(
         functools.partial(relax_kernel, owners),
         out_shape=jax.ShapeDtypeStruct(field.shape, f32),
-        in_specs=[VMEM] * 6,
+        in_specs=[VMEM] * 4,
         out_specs=HBM,
         scratch_shapes=[
-            pltpu.VMEM(((planes + 2) * rows_count * 8 + 8, LANES), f32),
-            pltpu.SMEM((owners + 8, LANES), i32),
+            pltpu.VMEM((sweep_rows + 8, LANES), f32),
+            pltpu.SMEM(codes.shape, i32),
+            pltpu.VMEM((2 * LANES * ROWS, LANES), f32),
             pltpu.VMEM(field.shape, f32),
             pltpu.SemaphoreType.DMA,
             pltpu.SemaphoreType.DMA((planes,)),
         ],
         compiler_params=params,
         name="relax",
-    )(
-        codes, field, below, following, time_ratio,
-        values.reshape(owners * 16, LANES),
-    )
+    )(rows, codes, time_ratio, values.reshape(owners * 16, LANES))
 
 
 def solution(mesh):

time: 34.5 us -> 33.3 us (0.965)
  blocking collectives: 0 us -> 9.29 us
  waiting for transfers between devices: 13.1 us -> 4.97 us
  starting transfers between devices: 11.7 us -> 8.27 us
  Pallas kernels: 9.33 us -> 10.4 us
    all_to_all x0 -> x1, blocking collectives: none -> 9.29 us  [on_device(): lax.all_to_all(values, 'grid', split_axis=0, concat_axis=0, tiled=True)]
    ppermute x2, waiting for transfers between devices: 3.86 us -> 0.01 us  [passed_along(): return lax.ppermute(value, axis, pairs)]
    all_to_all x1 -> x0, starting transfers between devices: 3.36 us -> none  [on_device(): lax.all_to_all(values, 'grid', split_axis=0, concat_axis=0, tiled=True)]
    all_to_all x1 -> x0, waiting for transfers between devices: 2.92 us -> none  [on_device(): lax.all_to_all(values, 'grid', split_axis=0, concat_axis=0, tiled=True)]
    pallas_call x1, Pallas kernels: 0.37 us -> 1.69 us  [on_device(): pl.pallas_call(table_kernel, out_shape=[jax.ShapeDtypeStruct(((planes + 1...]
    all_to_all x1, waiting for transfers between devices: 6.27 us -> 4.96 us  [on_device(): lax.all_to_all(message, 'grid', split_axis=0, concat_axis=0, tiled=True)]
    pallas_call x1, Pallas kernels: 3.16 us -> 2.59 us  [on_device(): pl.pallas_call(functools.partial(gather_kernel, owners), out_shape=jax.Sh...]
    pallas_call x1, Pallas kernels: 4.04 us -> 4.45 us  [on_device(): pl.pallas_call(functools.partial(relax_kernel, owners), out_shape=jax.Sha...]
  transfers between devices with their start and end apart: 4 -> 3, of which waited for: 3 -> 1; matrix products, arithmetic and copies ran while one was open for 0% -> 0% of each run, Pallas kernels for 1% -> 5%
where the time goes in v1:
time: 33.3 us; the launch traced here: 33 us
  Pallas kernels  10.4 us (31%)
  blocking collectives  9.29 us (28%)
  starting transfers between devices  8.27 us (25%)
  waiting for transfers between devices  4.97 us (15%)
    all_to_all x1, blocking collectives, on_device(): lax.all_to_all(values, 'grid', split_axis=0, concat_axis=0, tiled=True)  9.29 us
    all_to_all x1, starting transfers between devices, on_device(): lax.all_to_all(message, 'grid', split_axis=0, concat_axis=0, tiled=True)  5.84 us
    all_to_all x1, waiting for transfers between devices, on_device(): lax.all_to_all(message, 'grid', split_axis=0, concat_axis=0, tiled=True)  4.96 us
    pallas_call x1, Pallas kernels, on_device(): pl.pallas_call(functools.partial(relax_kernel, owners), out_shape=jax.Sha...  4.45 us
    pallas_call x1, Pallas kernels, on_device(): pl.pallas_call(functools.partial(gather_kernel, owners), out_shape=jax.Sh...  2.59 us
    ppermute x2, starting transfers between devices, passed_along(): return lax.ppermute(value, axis, pairs)  2.43 us
    pallas_call x1, Pallas kernels, on_device(): pl.pallas_call(table_kernel, out_shape=[jax.ShapeDtypeStruct(((planes + 1...  1.69 us
    pallas_call x1, Pallas kernels, on_device(): pl.pallas_call(first_kernel, out_shape=[jax.ShapeDtypeStruct((owners, 8,...  1.68 us
  transfers between devices with their start and end apart: 3, of which 1 were waited for; matrix products, arithmetic and copies ran while one was open for 0% of the time, Pallas kernels for 5%

profile of v1, /device:TPU:0, one launch (start us, length us, event | category | flops | bytes accessed | tf_op | source)
XLA Modules:
  0.0 33.0 jit_solution(17854998335422860728)
XLA Ops:
  0.0 1.7 %first.1 = (f32[8,8,128]{2,1,0:T(8,128)}, s32[2,16,128]{2,1,0:T(8,128)S(1)}, f32[8,1,32,128]{3,2,1,0:T(8,128)S(1)}, f32[5,1,32,128]{3,2,1,0:T(8,128)S(1)}) custom-call(s32[1,8]{1,0:T(1,128)} %count_ref.1, s32[1,8,2,128]{3,2,1,0:T(2,128)} %cell_ref.1, f32[1,8,3,2,128]{4,3,2,1,0:T(2,128)} %bitcast.7, s32[1,8,2,128]{3,2,1,0:T(2,128)} %node_ref.1, ...), custom_call_target="tpu_custom_call" | custom-call | tf_op jit(solution)/shard_map/first/pallas_call | solution.py:385
  1.7 2.4 %collective-permute-start = (f32[8,1,32,128]{3,2,1,0:T(8,128)S(1)}, f32[8,1,32,128]{3,2,1,0:T(8,128)S(1)}, u32[]{:S(2)}, u32[]{:S(2)}) collective-permute-start(f32[8,1,32,128]{3,2,1,0:T(8,128)S(1)} %get-tuple-element.11), channel_id=1, source_target_pairs={{0,3},{1,0},{2,1},{3,2},{4,7},{5,4},{6,5},{7,6},{8,11},{9,8},{10,9... | collective-permute-start | bytes 393224 | tf_op jit(solution)/shard_map/ppermute | solution.py:20
  4.1 0.0 collective-permute-start.1
  4.1 5.8 %all-to-all-start = ((f32[8,8,128]{2,1,0:T(8,128)}), f32[8,8,128]{2,1,0:T(8,128)S(1)}, u32[]{:S(2)}, u32[]{:S(2)}) async-start(f32[8,8,128]{2,1,0:T(8,128)} %get-tuple-element.16), calls=%async_computation | async-start | bytes 65536 | tf_op jit(solution)/shard_map/all_to_all | solution.py:410
  10.0 0.0 copy-start
  10.0 0.0 collective-permute-done.1.below_ref
  10.0 0.0 collective-permute-done.next_ref
  10.0 1.7 %table.1 = (f32[2304,128]{1,0:T(8,128)S(1)}, f32[2560,128]{1,0:T(8,128)S(1)}) custom-call(f32[5,8,32,128]{3,2,1,0:T(8,128)} %field_ref.3, f32[3,8,32,128]{3,2,1,0:T(8,128)} %jitter_ref.3, f32[8,1,32,128]{3,2,1,0:T(8,128)S(1)} %collective-permute-done.next_ref, f32[5,1,32,128]{3,2,1,0:T(8,128)S(1)} %collective-permute-done.1.below_ref), custom_call_target="tpu_custom_call" | custom-call | bytes 8388608 | tf_op jit(solution)/shard_map/table/pallas_call | solution.py:412
  11.7 5.0 %all-to-all-done = f32[8,8,128]{2,1,0:T(8,128)S(1)} async-done(((f32[8,8,128]{2,1,0:T(8,128)}), f32[8,8,128]{2,1,0:T(8,128)S(1)}, u32[]{:S(2)}, u32[]{:S(2)}) %all-to-all-start) | async-done | bytes 32800 | tf_op jit(solution)/shard_map/all_to_all | solution.py:410
  16.6 2.6 %gather.1 = f32[128,128]{1,0:T(8,128)S(1)} custom-call(f32[2304,128]{1,0:T(8,128)S(1)} %get-tuple-element.15.table_ref, f32[64,128]{1,0:T(8,128)S(1)} %bitcast.6), custom_call_target="tpu_custom_call" | custom-call | tf_op jit(solution)/shard_map/gather/pallas_call | solution.py:429
  19.2 9.3 %all_to_all.10 = f32[8,16,128]{2,1,0:T(8,128)S(1)} all-to-all(f32[8,16,128]{2,1,0:T(8,128)S(1)} %bitcast.5), channel_id=1, replica_groups=mesh['grid'=8,'sub'=4] {'grid'}, dimensions={0} | all-to-all | bytes 131072 | tf_op jit(solution)/shard_map/all_to_all | solution.py:445
  28.5 0.0 copy-done
  28.5 4.5 %relax.1 = f32[5,8,32,128]{3,2,1,0:T(8,128)} custom-call(f32[2560,128]{1,0:T(8,128)S(1)} %get-tuple-element.13.rows_ref, s32[2,16,128]{2,1,0:T(8,128)S(1)} %get-tuple-element.14.code_ref, f32[8,32,128]{2,1,0:T(8,128)S(1)} %copy-done, f32[128,128]{1,0:T(8,128)S(1)} %bitcast.4), custom_call_target="tpu_custom_call" | custom-call | tf_op jit(solution)/shard_map/relax/pallas_call | solution.py:446
Async XLA Ops:
  1.7 8.3 %collective-permute-start = (f32[8,1,32,128]{3,2,1,0:T(8,128)S(1)}, f32[8,1,32,128]{3,2,1,0:T(8,128)S(1)}, u32[]{:S(2)}, u32[]{:S(2)}) collective-permute-start(f32[8,1,32,128]{3,2,1,0:T(8,128)S(1)} %get-tuple-element.11), channel_id=1, source_target_pairs={{0,3},{1,0},{2,1},{3,2},{4,7},{5,4},{6,5},{7,6},{8,11},{9,8},{10,9... | collective-permute-start | bytes 393224 | tf_op jit(solution)/shard_map/ppermute | solution.py:20
  4.1 5.8 %collective-permute-start.1 = (f32[5,1,32,128]{3,2,1,0:T(8,128)S(1)}, f32[5,1,32,128]{3,2,1,0:T(8,128)S(1)}, u32[]{:S(2)}, u32[]{:S(2)}) collective-permute-start(f32[5,1,32,128]{3,2,1,0:T(8,128)S(1)} %get-tuple-element.12), channel_id=1, source_target_pairs={{0,1},{1,2},{2,3},{3,0},{4,5},{5,6},{6,7},{7,4},{8,9},{9,10},{10,1... | collective-permute-start | bytes 245768 | tf_op jit(solution)/shard_map/ppermute | solution.py:20
  4.1 12.5 %all-to-all-start = ((f32[8,8,128]{2,1,0:T(8,128)}), f32[8,8,128]{2,1,0:T(8,128)S(1)}, u32[]{:S(2)}, u32[]{:S(2)}) async-start(f32[8,8,128]{2,1,0:T(8,128)} %get-tuple-element.16), calls=%async_computation | async-start | bytes 65536 | tf_op jit(solution)/shard_map/all_to_all | solution.py:410
  10.0 18.6 %copy-start = (f32[8,32,128]{2,1,0:T(8,128)S(1)}, f32[8,32,128]{2,1,0:T(8,128)}, u32[]{:S(2)}) copy-start(f32[8,32,128]{2,1,0:T(8,128)} %ratio_ref.1) | copy-start | bytes 393220

commit v2 on v1

--- a/solution.py
+++ b/solution.py
@@ -50,8 +50,8 @@
     lane = lax.broadcasted_iota(jnp.int32, (1, points), 1)
 
     def code(place, nodes, live):
-        code_ref[0, place, :] = jnp.where(live, (nodes >> 7) * 8, spare)
-        code_ref[1, place, :] = ((nodes & 127) - lane) & 127
+        code_ref[pl.ds(place, 1), :] = jnp.where(live, (nodes >> 7) * 8, spare)
+        code_ref[pl.ds(owners + 1 + place, 1), :] = ((nodes & 127) - lane) & 127
 
     def one(owner, carry):
         count = count_smem[0, owner]
@@ -64,11 +64,11 @@
             message_ref[owner, 1 + c : 2 + c, :] = offset_vmem[0, owner, c, 0:1, :]
             message_ref[owner, 5 + c : 6 + c, :] = offset_vmem[0, owner, c, 1:2, :]
         nodes = node_vmem[0, owner]
-        code(pl.ds(owner, 1), nodes[0:1], lane < count)
+        code(owner, nodes[0:1], lane < count)
 
         @pl.when(more)
         def _():
-            code(pl.ds(owners, 1), nodes[1:2], lane + points < count)
+            code(owners, nodes[1:2], lane + points < count)
 
         return carry
 
@@ -129,39 +129,19 @@
     return values
 
 
-def table_kernel(
-    field_ref, jitter_ref, next_ref, below_ref, table_ref, rows_ref, field, jitter, sem
-):
-    variables, planes, rows_count, columns = field_ref.shape
-    copies = [
-        pltpu.make_async_copy(field_ref, field, sem.at[0]),
-        pltpu.make_async_copy(jitter_ref, jitter, sem.at[1]),
-    ]
-    for copy in copies:
-        copy.start()
-
-    def one_plane(plane, read):
+def lay_out(table, field_ref, jitter_ref, next_ref):
+    planes, columns = field_ref.shape[1], field_ref.shape[3]
+
+    def read(plane, variable):
+        if plane == planes:
+            return next_ref[variable, 0]
+        return jitter_ref[variable, plane] if variable < 3 else field_ref[variable - 3, plane]
+
+    for plane in range(planes + 1):
         for half in range(2):
-            tile = jnp.concatenate([read(4 * half + w) for w in range(4)], 0).T
+            tile = jnp.concatenate([read(plane, 4 * half + w) for w in range(4)], 0).T
             first = plane * (2 * columns) + half
-            table_ref[pl.ds(first, columns, stride=2), :] = tile
-
-    def put(plane, variable, tile):
-        first = plane * rows_count * 8 + variable
-        rows_ref[pl.ds(first, rows_count, stride=8), :] = tile
-
-    one_plane(planes, lambda v: next_ref[v, 0])
-    for variable in range(variables):
-        put(0, variable, below_ref[variable, 0])
-        put(planes + 1, variable, next_ref[3 + variable, 0])
-    for plane in range(planes):
-        put(plane + 1, variables, jnp.zeros((rows_count, columns), jnp.float32))
-    for copy in copies:
-        copy.wait()
-    for plane in range(planes):
-        one_plane(plane, lambda v: jitter[v, plane] if v < 3 else field[v - 3, plane])
-        for variable in range(variables):
-            put(plane + 1, variable, field[variable, plane])
+            table[pl.ds(first, columns, stride=2), :] = tile
 
 
 def separated(tiles, lane):
@@ -191,7 +171,10 @@
         lax.fori_loop(0, owners + 1, body, 0)
 
 
-def gather_kernel(owners, table_ref, message_ref, out_ref, decoded, codes, picked, parts, sem):
+def gather_kernel(
+    owners, field_ref, jitter_ref, next_ref, message_ref, out_ref,
+    table, decoded, codes, picked, parts, sem,
+):
     rows_count = 32
     me = lax.axis_index("grid")
     heavy = lax.rem(me + owners - 1, owners)
@@ -211,6 +194,7 @@
     decode(more, pl.ds(owners, ROWS))
     copy = pltpu.make_async_copy(decoded, codes, sem)
     copy.start()
+    lay_out(table, field_ref, jitter_ref, next_ref)
     copy.wait()
 
     low = sublane < 4
@@ -224,8 +208,8 @@
                 row = code >> 7
                 tile = jnp.where(
                     low,
-                    table_ref[pl.ds(row, ROWS), :],
-                    table_ref[pl.ds(row + (2 * LANES - 4), ROWS), :],
+                    table[pl.ds(row, ROWS), :],
+                    table[pl.ds(row + (2 * LANES - 4), ROWS), :],
                 )
                 tile = pltpu.roll(tile, code & 127, 1)
                 k2 = k & 1
@@ -277,8 +261,8 @@
 
 
 def relax_kernel(
-    owners, rows_ref, code_ref, ratio_ref, values_ref, out_ref, table, codes, rolled, out_vmem,
-    sem, out_sem,
+    owners, code_ref, field_ref, next_ref, below_ref, ratio_ref, values_ref, out_ref,
+    table, codes, rolled, out_vmem, sem, out_sem,
 ):
     variables, planes, rows_count, _ = out_ref.shape
     width = 8
@@ -289,9 +273,17 @@
     lane = lax.broadcasted_iota(jnp.int32, (ROWS, LANES), 1)
     sublane = lax.broadcasted_iota(jnp.int32, (ROWS, LANES), 0)
     heavy = lax.rem(lax.axis_index("grid") + 1, owners)
-    for plane in range(planes + 2):
-        place = pl.ds(plane * plane_rows, plane_rows)
-        table[place, :] = rows_ref[place, :]
+
+    def put(plane, variable, tile):
+        table[pl.ds(plane * plane_rows + variable, rows_count, stride=width), :] = tile
+
+    for variable in range(variables):
+        put(0, variable, below_ref[variable, 0])
+        put(planes + 1, variable, next_ref[3 + variable, 0])
+        for plane in range(planes):
+            put(plane + 1, variable, field_ref[variable, plane])
+    for plane in range(planes):
+        put(plane + 1, variables, jnp.zeros((rows_count, LANES), jnp.float32))
     copy.wait()
 
     def rotate(source, half):
@@ -305,13 +297,13 @@
         tile = jnp.where(sublane == variables + 1, lane.astype(jnp.float32), tile)
         for point in range(LANES):
             place = (half * LANES + point) * ROWS
-            rolled[place : place + ROWS, :] = pltpu.roll(tile, codes[1, source, point], 1)
+            rolled[place : place + ROWS, :] = pltpu.roll(tile, codes[owners + 1 + source, point], 1)
 
     def store(source, half):
         for point in range(LANES):
             place = (half * LANES + point) * ROWS
             tag = rolled[place + variables + 1 : place + variables + 2, :]
-            row = pl.multiple_of(codes[0, source, point] + plane_rows, width)
+            row = pl.multiple_of(codes[source, point] + plane_rows, width)
             pltpu.store(
                 table.at[pl.ds(row, width), :],
                 rolled[place : place + ROWS, :],
@@ -322,8 +314,8 @@
         rotate(0, 0)
         for source in range(owners + 1):
             if source < owners:
-                rotate(source + 1, (source + 1) % 2)
-            store(source, source % 2)
+                rotate(source + 1, source + 1)
+            store(source, source)
     else:
 
         def one_source(source, carry):
@@ -378,15 +370,12 @@
     owners, points = donor_cell.shape[1], donor_cell.shape[3]
     params = pltpu.CompilerParams(vmem_limit_bytes=LIMIT)
     offsets = jnp.swapaxes(receptor_offset, 2, 3)
-    field, node_jitter = (
-        pltpu.with_memory_space_constraint(x, pltpu.HBM) for x in (field, node_jitter)
-    )
     f32, i32 = jnp.float32, jnp.int32
     message, codes, first, last = pl.pallas_call(
         first_kernel,
         out_shape=[
             jax.ShapeDtypeStruct((owners, 8, LANES), f32),
-            jax.ShapeDtypeStruct((2, owners + 8, LANES), i32),
+            jax.ShapeDtypeStruct((2 * owners + 8, LANES), i32),
             jax.ShapeDtypeStruct((3 + variables, 1, rows_count, cols_count), f32),
             jax.ShapeDtypeStruct((variables, 1, rows_count, cols_count), f32),
         ],
@@ -403,35 +392,21 @@
         name="first",
     )(*[
         pltpu.with_memory_space_constraint(x, pltpu.HBM)
-        for x in (point_count, donor_cell, offsets, receptor_node)
-    ], field, node_jitter)
+        for x in (point_count, donor_cell, offsets, receptor_node, field, node_jitter)
+    ])
+    field, node_jitter, time_ratio, message = lax.optimization_barrier(
+        (field, node_jitter, time_ratio, message)
+    )
     following = passed_along(first, "sub", -1)
     below = passed_along(last, "sub", 1)
     message = lax.all_to_all(message, "grid", split_axis=0, concat_axis=0, tiled=True)
-    sweep_rows = (planes + 2) * rows_count * 8
-    table, rows = pl.pallas_call(
-        table_kernel,
-        out_shape=[
-            jax.ShapeDtypeStruct(((planes + 1) * cols_count * 2, LANES), f32),
-            jax.ShapeDtypeStruct((sweep_rows, LANES), f32),
-        ],
-        in_specs=[HBM, HBM, VMEM, VMEM],
-        out_specs=[VMEM, VMEM],
-        scratch_shapes=[
-            pltpu.VMEM(field.shape, f32),
-            pltpu.VMEM(node_jitter.shape, f32),
-            pltpu.SemaphoreType.DMA((2,)),
-        ],
-        compiler_params=params,
-        cost_estimate=pl.CostEstimate(flops=0, bytes_accessed=8 << 20, transcendentals=0),
-        name="table",
-    )(field, node_jitter, following, below)
     values = pl.pallas_call(
         functools.partial(gather_kernel, owners),
         out_shape=jax.ShapeDtypeStruct((owners * 16, LANES), f32),
-        in_specs=[VMEM, VMEM],
+        in_specs=[VMEM] * 4,
         out_specs=VMEM,
         scratch_shapes=[
+            pltpu.VMEM(((planes + 1) * cols_count * 2, LANES), f32),
             pltpu.VMEM((owners + 8, LANES), i32),
             pltpu.SMEM((owners + 8, LANES), i32),
             pltpu.VMEM((8 * (owners + 1) * 8, LANES), f32),
@@ -440,25 +415,25 @@
         ],
         compiler_params=params,
         name="gather",
-    )(table, message.reshape(owners * 8, LANES))
+    )(field, node_jitter, following, message.reshape(owners * 8, LANES))
     values = values.reshape(owners, 16, LANES)
     values = lax.all_to_all(values, "grid", split_axis=0, concat_axis=0, tiled=True)
     return pl.pallas_call(
         functools.partial(relax_kernel, owners),
         out_shape=jax.ShapeDtypeStruct(field.shape, f32),
-        in_specs=[VMEM] * 4,
+        in_specs=[VMEM] * 6,
         out_specs=HBM,
         scratch_shapes=[
-            pltpu.VMEM((sweep_rows + 8, LANES), f32),
+            pltpu.VMEM(((planes + 2) * rows_count * 8 + 8, LANES), f32),
             pltpu.SMEM(codes.shape, i32),
-            pltpu.VMEM((2 * LANES * ROWS, LANES), f32),
+            pltpu.VMEM(((owners + 1 if owners <= 8 else 1) * LANES * ROWS, LANES), f32),
             pltpu.VMEM(field.shape, f32),
             pltpu.SemaphoreType.DMA,
             pltpu.SemaphoreType.DMA((planes,)),
         ],
         compiler_params=params,
         name="relax",
-    )(rows, codes, time_ratio, values.reshape(owners * 16, LANES))
+    )(codes, field, following, below, time_ratio, values.reshape(owners * 16, LANES))
 
 
 def solution(mesh):

time: 33.3 us -> 33.8 us (1.015)
  blocking collectives: 9.29 us -> 12.3 us
  starting transfers between devices: 8.27 us -> 5.98 us
  Pallas kernels: 10.4 us -> 8.42 us
  waiting for transfers between devices: 4.97 us -> 6.78 us
    ppermute x2, waiting for transfers between devices: 0.01 us -> 3.86 us  [passed_along(): return lax.ppermute(value, axis, pairs)]
    all_to_all x1, blocking collectives: 9.29 us -> 12.3 us  [on_device(): lax.all_to_all(message, 'grid', split_axis=0, concat_axis=0, tiled=True)]
    all_to_all x1, starting transfers between devices: 5.84 us -> 3.5 us  [on_device(): lax.all_to_all(values, 'grid', split_axis=0, concat_axis=0, tiled=True)]
    all_to_all x1, waiting for transfers between devices: 4.96 us -> 2.92 us  [on_device(): lax.all_to_all(values, 'grid', split_axis=0, concat_axis=0, tiled=True)]
    pallas_call x1 -> x0, Pallas kernels: 1.69 us -> none  [on_device(): pl.pallas_call(table_kernel, out_shape=[jax.ShapeDtypeStruct(((planes + 1...]
    pallas_call x1, Pallas kernels: 2.59 us -> 3.43 us  [on_device(): pl.pallas_call(functools.partial(gather_kernel, owners), out_shape=jax.Sh...]
    pallas_call x1, Pallas kernels: 4.45 us -> 3.84 us  [on_device(): pl.pallas_call(functools.partial(relax_kernel, owners), out_shape=jax.Sha...]
    pallas_call x1, Pallas kernels: 1.68 us -> 1.15 us  [on_device(): pl.pallas_call(first_kernel, out_shape=[jax.ShapeDtypeStruct((owners, 8,...]
  transfers between devices with their start and end apart: 3 -> 3, of which waited for: 1 -> 2; matrix products, arithmetic and copies ran while one was open for 0% -> 0% of each run, Pallas kernels for 5% -> 0%
where the time goes in v2:
time: 33.8 us; the launch traced here: 33.6 us
  blocking collectives  12.3 us (36%)
  Pallas kernels  8.42 us (25%)
  waiting for transfers between devices  6.78 us (20%)
  starting transfers between devices  5.98 us (18%)
    all_to_all x1, blocking collectives, on_device(): lax.all_to_all(message, 'grid', split_axis=0, concat_axis=0, tiled=True)  12.3 us
    ppermute x2, waiting for transfers between devices, passed_along(): return lax.ppermute(value, axis, pairs)  3.86 us
    pallas_call x1, Pallas kernels, on_device(): pl.pallas_call(functools.partial(relax_kernel, owners), out_shape=jax.Sha...  3.84 us
    all_to_all x1, starting transfers between devices, on_device(): lax.all_to_all(values, 'grid', split_axis=0, concat_axis=0, tiled=True)  3.5 us
    pallas_call x1, Pallas kernels, on_device(): pl.pallas_call(functools.partial(gather_kernel, owners), out_shape=jax.Sh...  3.43 us
    all_to_all x1, waiting for transfers between devices, on_device(): lax.all_to_all(values, 'grid', split_axis=0, concat_axis=0, tiled=True)  2.92 us
    ppermute x2, starting transfers between devices, passed_along(): return lax.ppermute(value, axis, pairs)  2.49 us
    pallas_call x1, Pallas kernels, on_device(): pl.pallas_call(first_kernel, out_shape=[jax.ShapeDtypeStruct((owners, 8,...  1.15 us
  transfers between devices with their start and end apart: 3, of which 2 were waited for; matrix products, arithmetic and copies ran while one was open for 0% of the time, Pallas kernels for 0%

profile of v2, /device:TPU:0, one launch (start us, length us, event | category | flops | bytes accessed | tf_op | source)
XLA Modules:
  0.0 33.6 jit_solution(6020280750379642080)
XLA Ops:
  0.0 0.0 copy-start
  0.0 0.0 copy-start.1
  0.0 1.1 %first.1 = (f32[8,8,128]{2,1,0:T(8,128)S(1)}, s32[24,128]{1,0:T(8,128)S(1)}, f32[8,1,32,128]{3,2,1,0:T(8,128)S(1)}, f32[5,1,32,128]{3,2,1,0:T(8,128)S(1)}) custom-call(s32[1,8]{1,0:T(1,128)} %count_ref.1, s32[1,8,2,128]{3,2,1,0:T(2,128)} %cell_ref.1, f32[1,8,3,2,128]{4,3,2,1,0:T(2,128)} %bitcast.6, s32[1,8,2,128]{3,2,1,0:T(2,128)} %node_ref.1, ...), custom_call_target="tpu_custom_call" | custom-call | tf_op jit(solution)/shard_map/first/pallas_call | solution.py:374
  1.2 2.4 %collective-permute-start = (f32[8,1,32,128]{3,2,1,0:T(8,128)S(1)}, f32[8,1,32,128]{3,2,1,0:T(8,128)S(1)}, u32[]{:S(2)}, u32[]{:S(2)}) collective-permute-start(f32[8,1,32,128]{3,2,1,0:T(8,128)S(1)} %get-tuple-element.16), channel_id=1, source_target_pairs={{0,3},{1,0},{2,1},{3,2},{4,7},{5,4},{6,5},{7,6},{8,11},{9,8},{10,9... | collective-permute-start | bytes 393224 | tf_op jit(solution)/shard_map/ppermute | solution.py:20
  3.6 12.3 %all_to_all.10 = f32[8,8,128]{2,1,0:T(8,128)S(1)} all-to-all(f32[8,8,128]{2,1,0:T(8,128)S(1)} %get-tuple-element.20), channel_id=1, replica_groups=mesh['grid'=8,'sub'=4] {'grid'}, dimensions={0} | all-to-all | bytes 65536 | tf_op jit(solution)/shard_map/all_to_all | solution.py:402
  15.9 0.0 collective-permute-done.next_ref
  15.9 0.0 copy-done
  15.9 0.0 copy-done.1
  15.9 3.4 %gather.1 = f32[128,128]{1,0:T(8,128)} custom-call(f32[5,8,32,128]{3,2,1,0:T(8,128)S(1)} %copy-done, f32[3,8,32,128]{3,2,1,0:T(8,128)S(1)} %copy-done.1, f32[8,1,32,128]{3,2,1,0:T(8,128)S(1)} %collective-permute-done.next_ref, f32[64,128]{1,0:T(8,128)S(1)} %bitcast.5), custom_call_target="tpu_custom_call" | custom-call | tf_op jit(solution)/shard_map/gather/pallas_call | solution.py:403
  19.3 0.0 copy-start.2
  19.4 3.5 %all-to-all-start.1 = ((f32[8,16,128]{2,1,0:T(8,128)}), f32[8,16,128]{2,1,0:T(8,128)S(1)}, u32[]{:S(2)}, u32[]{:S(2)}) async-start(f32[8,16,128]{2,1,0:T(8,128)} %bitcast.2), calls=%async_computation.1 | async-start | bytes 131072 | tf_op jit(solution)/shard_map/all_to_all | solution.py:420
  22.9 0.1 collective-permute-start.1
  22.9 3.9 %collective-permute-done.1.below_ref = f32[5,1,32,128]{3,2,1,0:T(8,128)S(1)} collective-permute-done((f32[5,1,32,128]{3,2,1,0:T(8,128)S(1)}, f32[5,1,32,128]{3,2,1,0:T(8,128)S(1)}, u32[]{:S(2)}, u32[]{:S(2)}) %collective-permute-start.1) | collective-permute-done | bytes 81952 | tf_op jit(solution)/shard_map/ppermute | solution.py:20
  26.8 2.9 %all-to-all-done.1 = f32[8,16,128]{2,1,0:T(8,128)S(1)} async-done(((f32[8,16,128]{2,1,0:T(8,128)}), f32[8,16,128]{2,1,0:T(8,128)S(1)}, u32[]{:S(2)}, u32[]{:S(2)}) %all-to-all-start.1) | async-done | bytes 65568 | tf_op jit(solution)/shard_map/all_to_all | solution.py:420
  29.7 0.0 copy-done.2
  29.7 3.8 %relax.1 = f32[5,8,32,128]{3,2,1,0:T(8,128)} custom-call(s32[24,128]{1,0:T(8,128)S(1)} %get-tuple-element.13.code_ref, f32[5,8,32,128]{3,2,1,0:T(8,128)S(1)} %copy-done, f32[8,1,32,128]{3,2,1,0:T(8,128)S(1)} %collective-permute-done.next_ref, f32[5,1,32,128]{3,2,1,0:T(8,128)S(1)} %collective-permute-done.1.below_ref, f32[8,32,128]{2,1,0:T(8,128)S(1)} %copy-done.2, ...), custom_call_target="tpu_custom_call" | custom-call | tf_op jit(solution)/shard_map/relax/pallas_call | solution.py:421
Async XLA Ops:
  0.0 15.9 %copy-start = (f32[5,8,32,128]{3,2,1,0:T(8,128)S(1)}, f32[5,8,32,128]{3,2,1,0:T(8,128)}, u32[]{:S(2)}) copy-start(f32[5,8,32,128]{3,2,1,0:T(8,128)} %field_ref.3) | copy-start | bytes 1966084
  0.0 15.9 %copy-start.1 = (f32[3,8,32,128]{3,2,1,0:T(8,128)S(1)}, f32[3,8,32,128]{3,2,1,0:T(8,128)}, u32[]{:S(2)}) copy-start(f32[3,8,32,128]{3,2,1,0:T(8,128)} %jitter_ref.2) | copy-start | bytes 1179652
  1.2 14.7 %collective-permute-start = (f32[8,1,32,128]{3,2,1,0:T(8,128)S(1)}, f32[8,1,32,128]{3,2,1,0:T(8,128)S(1)}, u32[]{:S(2)}, u32[]{:S(2)}) collective-permute-start(f32[8,1,32,128]{3,2,1,0:T(8,128)S(1)} %get-tuple-element.16), channel_id=1, source_target_pairs={{0,3},{1,0},{2,1},{3,2},{4,7},{5,4},{6,5},{7,6},{8,11},{9,8},{10,9... | collective-permute-start | bytes 393224 | tf_op jit(solution)/shard_map/ppermute | solution.py:20
  19.3 10.4 %copy-start.2 = (f32[8,32,128]{2,1,0:T(8,128)S(1)}, f32[8,32,128]{2,1,0:T(8,128)}, u32[]{:S(2)}) copy-start(f32[8,32,128]{2,1,0:T(8,128)} %ratio_ref) | copy-start | bytes 393220
  19.4 10.3 %all-to-all-start.1 = ((f32[8,16,128]{2,1,0:T(8,128)}), f32[8,16,128]{2,1,0:T(8,128)S(1)}, u32[]{:S(2)}, u32[]{:S(2)}) async-start(f32[8,16,128]{2,1,0:T(8,128)} %bitcast.2), calls=%async_computation.1 | async-start | bytes 131072 | tf_op jit(solution)/shard_map/all_to_all | solution.py:420
  22.9 3.9 %collective-permute-start.1 = (f32[5,1,32,128]{3,2,1,0:T(8,128)S(1)}, f32[5,1,32,128]{3,2,1,0:T(8,128)S(1)}, u32[]{:S(2)}, u32[]{:S(2)}) collective-permute-start(f32[5,1,32,128]{3,2,1,0:T(8,128)S(1)} %get-tuple-element.17), channel_id=1, source_target_pairs={{0,1},{1,2},{2,3},{3,0},{4,5},{5,6},{6,7},{7,4},{8,9},{9,10},{10,1... | collective-permute-start | bytes 245768 | tf_op jit(solution)/shard_map/ppermute | solution.py:20

commit v3 on v2

--- a/solution.py
+++ b/solution.py
@@ -163,6 +163,14 @@
     return pl.ds(first if isinstance(first, int) else pl.multiple_of(first, ROWS), ROWS)
 
 
+def after(me, body):
+    def once(step, carry):
+        body()
+        return carry
+
+    lax.fori_loop(0, jnp.minimum(me + 1, 1), once, 0)
+
+
 def each_source(owners, body):
     if owners <= 8:
         for source in range(owners + 1):
@@ -172,7 +180,7 @@
 
 
 def gather_kernel(
-    owners, field_ref, jitter_ref, next_ref, message_ref, out_ref,
+    owners, field_ref, jitter_ref, next_ref, below_ref, message_ref, out_ref,
     table, decoded, codes, picked, parts, sem,
 ):
     rows_count = 32
@@ -194,7 +202,7 @@
     decode(more, pl.ds(owners, ROWS))
     copy = pltpu.make_async_copy(decoded, codes, sem)
     copy.start()
-    lay_out(table, field_ref, jitter_ref, next_ref)
+    after(me, lambda: lay_out(table, field_ref, jitter_ref, next_ref))
     copy.wait()
 
     low = sublane < 4
@@ -272,18 +280,22 @@
     copy.start()
     lane = lax.broadcasted_iota(jnp.int32, (ROWS, LANES), 1)
     sublane = lax.broadcasted_iota(jnp.int32, (ROWS, LANES), 0)
-    heavy = lax.rem(lax.axis_index("grid") + 1, owners)
+    me = lax.axis_index("grid")
+    heavy = lax.rem(me + 1, owners)
 
     def put(plane, variable, tile):
         table[pl.ds(plane * plane_rows + variable, rows_count, stride=width), :] = tile
 
-    for variable in range(variables):
-        put(0, variable, below_ref[variable, 0])
-        put(planes + 1, variable, next_ref[3 + variable, 0])
+    def put_all():
+        for variable in range(variables):
+            put(0, variable, below_ref[variable, 0])
+            put(planes + 1, variable, next_ref[3 + variable, 0])
+            for plane in range(planes):
+                put(plane + 1, variable, field_ref[variable, plane])
         for plane in range(planes):
-            put(plane + 1, variable, field_ref[variable, plane])
-    for plane in range(planes):
-        put(plane + 1, variables, jnp.zeros((rows_count, LANES), jnp.float32))
+            put(plane + 1, variables, jnp.zeros((rows_count, LANES), jnp.float32))
+
+    after(me, put_all)
     copy.wait()
 
     def rotate(source, half):
@@ -394,16 +406,13 @@
         pltpu.with_memory_space_constraint(x, pltpu.HBM)
         for x in (point_count, donor_cell, offsets, receptor_node, field, node_jitter)
     ])
-    field, node_jitter, time_ratio, message = lax.optimization_barrier(
-        (field, node_jitter, time_ratio, message)
-    )
     following = passed_along(first, "sub", -1)
     below = passed_along(last, "sub", 1)
     message = lax.all_to_all(message, "grid", split_axis=0, concat_axis=0, tiled=True)
     values = pl.pallas_call(
         functools.partial(gather_kernel, owners),
         out_shape=jax.ShapeDtypeStruct((owners * 16, LANES), f32),
-        in_specs=[VMEM] * 4,
+        in_specs=[VMEM] * 5,
         out_specs=VMEM,
         scratch_shapes=[
             pltpu.VMEM(((planes + 1) * cols_count * 2, LANES), f32),
@@ -415,7 +424,7 @@
         ],
         compiler_params=params,
         name="gather",
-    )(field, node_jitter, following, message.reshape(owners * 8, LANES))
+    )(field, node_jitter, following, below, message.reshape(owners * 8, LANES))
     values = values.reshape(owners, 16, LANES)
     values = lax.all_to_all(values, "grid", split_axis=0, concat_axis=0, tiled=True)
     return pl.pallas_call(

time: 33.8 us -> 32 us (0.947)
  blocking collectives: 12.3 us -> 21.7 us
  waiting for transfers between devices: 6.78 us -> 0.01 us
  starting transfers between devices: 5.98 us -> 2.43 us
  Pallas kernels: 8.42 us -> 7.57 us
    all_to_all x0 -> x1, blocking collectives: none -> 9.42 us  [on_device(): lax.all_to_all(values, 'grid', split_axis=0, concat_axis=0, tiled=True)]
    ppermute x2, waiting for transfers between devices: 3.86 us -> 0.01 us  [passed_along(): return lax.ppermute(value, axis, pairs)]
    all_to_all x1 -> x0, starting transfers between devices: 3.5 us -> none  [on_device(): lax.all_to_all(values, 'grid', split_axis=0, concat_axis=0, tiled=True)]
    all_to_all x1 -> x0, waiting for transfers between devices: 2.92 us -> none  [on_device(): lax.all_to_all(values, 'grid', split_axis=0, concat_axis=0, tiled=True)]
    pallas_call x1, Pallas kernels: 3.43 us -> 2.6 us  [on_device(): pl.pallas_call(functools.partial(gather_kernel, owners), out_shape=jax.Sh...]
  transfers between devices with their start and end apart: 3 -> 2, of which waited for: 2 -> 0; matrix products, arithmetic and copies ran while one was open for 0% -> 0% of each run, Pallas kernels for 0% -> 0%
where the time goes in v3:
time: 32 us; the launch traced here: 31.8 us
  blocking collectives  21.7 us (68%)
  Pallas kernels  7.57 us (24%)
  starting transfers between devices  2.43 us (8%)
    all_to_all x1, blocking collectives, on_device(): lax.all_to_all(message, 'grid', split_axis=0, concat_axis=0, tiled=True)  12.3 us
    all_to_all x1, blocking collectives, on_device(): lax.all_to_all(values, 'grid', split_axis=0, concat_axis=0, tiled=True)  9.42 us
    pallas_call x1, Pallas kernels, on_device(): pl.pallas_call(functools.partial(relax_kernel, owners), out_shape=jax.Sha...  3.82 us
    pallas_call x1, Pallas kernels, on_device(): pl.pallas_call(functools.partial(gather_kernel, owners), out_shape=jax.Sh...  2.6 us
    ppermute x2, starting transfers between devices, passed_along(): return lax.ppermute(value, axis, pairs)  2.43 us
    pallas_call x1, Pallas kernels, on_device(): pl.pallas_call(first_kernel, out_shape=[jax.ShapeDtypeStruct((owners, 8,...  1.15 us
  transfers between devices with their start and end apart: 2, of which 0 were waited for; matrix products, arithmetic and copies ran while one was open for 0% of the time, Pallas kernels for 0%

profile of v3, /device:TPU:0, one launch (start us, length us, event | category | flops | bytes accessed | tf_op | source)
XLA Modules:
  0.0 31.8 jit_solution(5129795021141542072)
XLA Ops:
  0.0 0.0 copy-start
  0.0 0.0 copy-start.1
  0.0 1.1 %first.1 = (f32[8,8,128]{2,1,0:T(8,128)S(1)}, s32[24,128]{1,0:T(8,128)S(1)}, f32[8,1,32,128]{3,2,1,0:T(8,128)S(1)}, f32[5,1,32,128]{3,2,1,0:T(8,128)S(1)}) custom-call(s32[1,8]{1,0:T(1,128)} %count_ref.1, s32[1,8,2,128]{3,2,1,0:T(2,128)} %cell_ref.1, f32[1,8,3,2,128]{4,3,2,1,0:T(2,128)} %bitcast.7, s32[1,8,2,128]{3,2,1,0:T(2,128)} %node_ref.1, ...), custom_call_target="tpu_custom_call" | custom-call | tf_op jit(solution)/shard_map/first/pallas_call | solution.py:386
  1.2 2.4 %collective-permute-start = (f32[8,1,32,128]{3,2,1,0:T(8,128)S(1)}, f32[8,1,32,128]{3,2,1,0:T(8,128)S(1)}, u32[]{:S(2)}, u32[]{:S(2)}) collective-permute-start(f32[8,1,32,128]{3,2,1,0:T(8,128)S(1)} %get-tuple-element.10), channel_id=1, source_target_pairs={{0,3},{1,0},{2,1},{3,2},{4,7},{5,4},{6,5},{7,6},{8,11},{9,8},{10,9... | collective-permute-start | bytes 393224 | tf_op jit(solution)/shard_map/ppermute | solution.py:20
  3.6 0.0 collective-permute-start.1
  3.6 12.3 %all_to_all.10 = f32[8,8,128]{2,1,0:T(8,128)S(1)} all-to-all(f32[8,8,128]{2,1,0:T(8,128)S(1)} %get-tuple-element.12), channel_id=1, replica_groups=mesh['grid'=8,'sub'=4] {'grid'}, dimensions={0} | all-to-all | bytes 65536 | tf_op jit(solution)/shard_map/all_to_all | solution.py:411
  15.9 0.0 collective-permute-done.1.below_ref
  15.9 0.0 collective-permute-done.next_ref
  15.9 0.0 copy-done
  15.9 0.0 copy-done.1
  15.9 2.6 %gather.1 = f32[128,128]{1,0:T(8,128)S(1)} custom-call(f32[5,8,32,128]{3,2,1,0:T(8,128)S(1)} %copy-done, f32[3,8,32,128]{3,2,1,0:T(8,128)S(1)} %copy-done.1, f32[8,1,32,128]{3,2,1,0:T(8,128)S(1)} %collective-permute-done.next_ref, f32[5,1,32,128]{3,2,1,0:T(8,128)S(1)} %collective-permute-done.1.below_ref, f32[64,128]{1,0:T(8,128)S(1)} %bitcast.6), custom_call_target="tpu_custom_call" | custom-call | tf_op jit(solution)/shard_map/gather/pallas_call | solution.py:412
  18.5 0.0 copy-start.2
  18.5 9.4 %all_to_all.11 = f32[8,16,128]{2,1,0:T(8,128)S(1)} all-to-all(f32[8,16,128]{2,1,0:T(8,128)S(1)} %bitcast.5), channel_id=1, replica_groups=mesh['grid'=8,'sub'=4] {'grid'}, dimensions={0} | all-to-all | bytes 131072 | tf_op jit(solution)/shard_map/all_to_all | solution.py:429
  28.0 0.0 copy-done.2
  28.0 3.8 %relax.1 = f32[5,8,32,128]{3,2,1,0:T(8,128)} custom-call(s32[24,128]{1,0:T(8,128)S(1)} %get-tuple-element.9.code_ref, f32[5,8,32,128]{3,2,1,0:T(8,128)S(1)} %copy-done, f32[8,1,32,128]{3,2,1,0:T(8,128)S(1)} %collective-permute-done.next_ref, f32[5,1,32,128]{3,2,1,0:T(8,128)S(1)} %collective-permute-done.1.below_ref, f32[8,32,128]{2,1,0:T(8,128)S(1)} %copy-done.2, ...), custom_call_target="tpu_custom_call" | custom-call | tf_op jit(solution)/shard_map/relax/pallas_call | solution.py:430
Async XLA Ops:
  0.0 15.9 %copy-start = (f32[5,8,32,128]{3,2,1,0:T(8,128)S(1)}, f32[5,8,32,128]{3,2,1,0:T(8,128)}, u32[]{:S(2)}) copy-start(f32[5,8,32,128]{3,2,1,0:T(8,128)} %field_ref.5) | copy-start | bytes 1966084
  0.0 15.9 %copy-start.1 = (f32[3,8,32,128]{3,2,1,0:T(8,128)S(1)}, f32[3,8,32,128]{3,2,1,0:T(8,128)}, u32[]{:S(2)}) copy-start(f32[3,8,32,128]{3,2,1,0:T(8,128)} %jitter_ref.3) | copy-start | bytes 1179652
  1.2 14.7 %collective-permute-start = (f32[8,1,32,128]{3,2,1,0:T(8,128)S(1)}, f32[8,1,32,128]{3,2,1,0:T(8,128)S(1)}, u32[]{:S(2)}, u32[]{:S(2)}) collective-permute-start(f32[8,1,32,128]{3,2,1,0:T(8,128)S(1)} %get-tuple-element.10), channel_id=1, source_target_pairs={{0,3},{1,0},{2,1},{3,2},{4,7},{5,4},{6,5},{7,6},{8,11},{9,8},{10,9... | collective-permute-start | bytes 393224 | tf_op jit(solution)/shard_map/ppermute | solution.py:20
  3.6 12.3 %collective-permute-start.1 = (f32[5,1,32,128]{3,2,1,0:T(8,128)S(1)}, f32[5,1,32,128]{3,2,1,0:T(8,128)S(1)}, u32[]{:S(2)}, u32[]{:S(2)}) collective-permute-start(f32[5,1,32,128]{3,2,1,0:T(8,128)S(1)} %get-tuple-element.11), channel_id=1, source_target_pairs={{0,1},{1,2},{2,3},{3,0},{4,5},{5,6},{6,7},{7,4},{8,9},{9,10},{10,1... | collective-permute-start | bytes 245768 | tf_op jit(solution)/shard_map/ppermute | solution.py:20
  18.5 9.4 %copy-start.2 = (f32[8,32,128]{2,1,0:T(8,128)S(1)}, f32[8,32,128]{2,1,0:T(8,128)}, u32[]{:S(2)}) copy-start(f32[8,32,128]{2,1,0:T(8,128)} %ratio_ref.1) | copy-start | bytes 393220

commit v4 on v3

--- a/solution.py
+++ b/solution.py
@@ -46,33 +46,30 @@
     for copy in copies[:4]:
         copy.wait()
 
-    spare = (planes + 1) * rows_count * 8
+    spare = planes * rows_count * 8
     lane = lax.broadcasted_iota(jnp.int32, (1, points), 1)
+
+    me = lax.axis_index("grid")
 
     def code(place, nodes, live):
         code_ref[pl.ds(place, 1), :] = jnp.where(live, (nodes >> 7) * 8, spare)
         code_ref[pl.ds(owners + 1 + place, 1), :] = ((nodes & 127) - lane) & 127
 
-    def one(owner, carry):
+    def one(distance, carry):
+        owner = lax.rem(me + distance, owners)
         count = count_smem[0, owner]
-        more = count > points
         cells = cell_vmem[0, owner].astype(jnp.float32)
-        counts = jnp.full((1, points), count, jnp.int32).astype(jnp.float32)
         message_ref[owner, 0:1, :] = cells[0:1]
-        message_ref[owner, 4:5, :] = jnp.where(more, cells[1:2], counts)
+        message_ref[owner, 4:5, :] = cells[1:2]
         for c in range(3):
             message_ref[owner, 1 + c : 2 + c, :] = offset_vmem[0, owner, c, 0:1, :]
             message_ref[owner, 5 + c : 6 + c, :] = offset_vmem[0, owner, c, 1:2, :]
-        nodes = node_vmem[0, owner]
-        code(owner, nodes[0:1], lane < count)
-
-        @pl.when(more)
-        def _():
-            code(owners, nodes[1:2], lane + points < count)
-
+        code(distance, node_vmem[0, owner, 0:1, :], lane < count)
         return carry
 
     lax.fori_loop(0, owners, one, 0, unroll=True)
+    heavy = lax.rem(me + 1, owners)
+    code(owners, node_vmem[0, heavy, 1:2, :], lane + points < count_smem[0, heavy])
     for copy in copies[4:]:
         copy.wait()
 
@@ -173,19 +170,23 @@
 
 def each_source(owners, body):
     if owners <= 8:
-        for source in range(owners + 1):
-            body(source, 0)
+        for distance in range(owners + 1):
+            body(distance, 1 if distance == 2 else LANES)
     else:
-        lax.fori_loop(0, owners + 1, body, 0)
+
+        def one(distance, carry):
+            body(distance, LANES)
+            return carry
+
+        lax.fori_loop(0, owners + 1, one, 0)
 
 
 def gather_kernel(
     owners, field_ref, jitter_ref, next_ref, below_ref, message_ref, out_ref,
-    table, decoded, codes, picked, parts, sem,
+    table, message, decoded, codes, picked, parts, answers, sem,
 ):
     rows_count = 32
     me = lax.axis_index("grid")
-    heavy = lax.rem(me + owners - 1, owners)
     lane = lax.broadcasted_iota(jnp.int32, (ROWS, LANES), 1)
     sublane = lax.broadcasted_iota(jnp.int32, (ROWS, LANES), 0)
 
@@ -195,10 +196,15 @@
         shift = ((lane & 30) - ((cells >> 7) & (rows_count - 1))) & 127
         decoded[place, :] = row * LANES + shift
 
+    def of_source(distance):
+        return lax.rem(me + owners - distance, owners)
+
+    for distance in range(owners):
+        message[tile_rows(distance), :] = message_ref[tile_rows(of_source(distance)), :]
     for block in range(owners // ROWS):
-        cells = message_ref[pl.ds(block * ROWS * 8, ROWS, stride=8), :]
+        cells = message[pl.ds(block * ROWS * 8, ROWS, stride=8), :]
         decode(cells, pl.ds(block * ROWS, ROWS))
-    more = jnp.broadcast_to(message_ref[pl.ds(heavy * 8 + 4, 1), :], (ROWS, LANES))
+    more = jnp.broadcast_to(message[12:13, :], (ROWS, LANES))
     decode(more, pl.ds(owners, ROWS))
     copy = pltpu.make_async_copy(decoded, codes, sem)
     copy.start()
@@ -208,10 +214,10 @@
     low = sublane < 4
     pairs = [(lane & 30) == 2 * k for k in range(16)]
 
-    def one_source(source, carry):
-        for block in range(4):
+    def one_source(source, points):
+        for block in range((points + 31) // 32):
             held = [None, None]
-            for k in range(32):
+            for k in range(min(32, points)):
                 code = codes[source, block * 32 + k]
                 row = code >> 7
                 tile = jnp.where(
@@ -222,9 +228,8 @@
                 tile = pltpu.roll(tile, code & 127, 1)
                 k2 = k & 1
                 held[k2] = tile if held[k2] is None else jnp.where(pairs[k >> 1], tile, held[k2])
-            for k in range(2):
+            for k in range(min(2, points)):
                 picked[tile_rows((2 * block + k) * (owners + 1) + source), :] = held[k]
-        return carry
 
     each_source(owners, one_source)
 
@@ -252,17 +257,20 @@
 
         target = []
         for c in range(3):
-            tile = message_ref[pl.ds(block * (ROWS * 8) + 1 + c, ROWS, stride=8), :]
+            tile = message[pl.ds(block * (ROWS * 8) + 1 + c, ROWS, stride=8), :]
             if last:
-                more = message_ref[pl.ds(heavy * 8 + 5 + c, 1), :]
+                more = message[13 + c : 14 + c, :]
                 tile = jnp.concatenate([tile, jnp.broadcast_to(more, (ROWS, LANES))], 0)
             target.append(tile)
         values = solve(corner, target)
         for variable in range(5):
-            place = pl.ds(block * (ROWS * 16) + variable, ROWS, stride=16)
-            out_ref[place, :] = values[variable][:ROWS]
+            answers[pl.ds(variable, ROWS, stride=8), :] = values[variable][:ROWS]
             if last:
-                out_ref[pl.ds(heavy * 16 + 8 + variable, 1), :] = values[variable][ROWS : ROWS + 1]
+                place = pl.ds(of_source(1) * 16 + 8 + variable, 1)
+                out_ref[place, :] = values[variable][ROWS : ROWS + 1]
+        for distance in range(ROWS):
+            source = of_source(block * ROWS + distance)
+            out_ref[tile_rows(2 * source), :] = answers[tile_rows(distance), :]
 
     for block in range(owners // ROWS):
         one_block(block, block == owners // ROWS - 1)
@@ -270,7 +278,7 @@
 
 def relax_kernel(
     owners, code_ref, field_ref, next_ref, below_ref, ratio_ref, values_ref, out_ref,
-    table, codes, rolled, out_vmem, sem, out_sem,
+    table, codes, rolled, plain, inverse, out_vmem, sem, out_sem,
 ):
     variables, planes, rows_count, _ = out_ref.shape
     width = 8
@@ -281,41 +289,40 @@
     lane = lax.broadcasted_iota(jnp.int32, (ROWS, LANES), 1)
     sublane = lax.broadcasted_iota(jnp.int32, (ROWS, LANES), 0)
     me = lax.axis_index("grid")
-    heavy = lax.rem(me + 1, owners)
-
-    def put(plane, variable, tile):
-        table[pl.ds(plane * plane_rows + variable, rows_count, stride=width), :] = tile
-
-    def put_all():
-        for variable in range(variables):
-            put(0, variable, below_ref[variable, 0])
-            put(planes + 1, variable, next_ref[3 + variable, 0])
-            for plane in range(planes):
-                put(plane + 1, variable, field_ref[variable, plane])
+
+    def lay_out_rows():
         for plane in range(planes):
-            put(plane + 1, variables, jnp.zeros((rows_count, LANES), jnp.float32))
-
-    after(me, put_all)
+            for variable in range(variables + 1):
+                tile = jnp.zeros((rows_count, LANES), jnp.float32)
+                if variable < variables:
+                    tile = field_ref[variable, plane]
+                first = plane * plane_rows + variable
+                table[pl.ds(first, rows_count, stride=width), :] = tile
+            inverse[plane] = 1.0 / (1.0 + 6.0 * ratio_ref[plane])
+
+    after(me, lay_out_rows)
     copy.wait()
 
-    def rotate(source, half):
-        if isinstance(source, int):
-            first = 16 * source if source < owners else heavy * 16 + 8
+    def rotate(distance, points, buffer):
+        if isinstance(distance, int):
+            owner = lax.rem(me + distance % owners + distance // owners, owners)
+            first = owner * 16 + 8 * (distance // owners)
         else:
-            first = jnp.where(source == owners, heavy * 16 + 8, source * 16)
-        if not isinstance(first, int):
-            first = pl.multiple_of(first, 8)
-        tile = jnp.where(sublane == variables, 1.0, values_ref[pl.ds(first, 8), :])
+            more = distance == owners
+            owner = lax.rem(jnp.where(more, me + 1, me + distance), owners)
+            first = owner * 16 + jnp.where(more, 8, 0)
+        tile = values_ref[pl.ds(pl.multiple_of(first, 8), 8), :]
+        tile = jnp.where(sublane == variables, 1.0, tile)
         tile = jnp.where(sublane == variables + 1, lane.astype(jnp.float32), tile)
-        for point in range(LANES):
-            place = (half * LANES + point) * ROWS
-            rolled[place : place + ROWS, :] = pltpu.roll(tile, codes[owners + 1 + source, point], 1)
-
-    def store(source, half):
-        for point in range(LANES):
-            place = (half * LANES + point) * ROWS
+        for point in range(points):
+            place = tile_rows(buffer * LANES + point)
+            rolled[place, :] = pltpu.roll(tile, codes[owners + 1 + distance, point], 1)
+
+    def store(distance, points, buffer):
+        for point in range(points):
+            place = (buffer * LANES + point) * ROWS
             tag = rolled[place + variables + 1 : place + variables + 2, :]
-            row = pl.multiple_of(codes[source, point] + plane_rows, width)
+            row = pl.multiple_of(codes[distance, point], width)
             pltpu.store(
                 table.at[pl.ds(row, width), :],
                 rolled[place : place + ROWS, :],
@@ -323,53 +330,68 @@
             )
 
     if owners <= 8:
-        rotate(0, 0)
-        for source in range(owners + 1):
-            if source < owners:
-                rotate(source + 1, source + 1)
-            store(source, source)
+        todo = []
+        each_source(owners, lambda distance, points: todo.append((distance, points, distance)))
+        rotate(*todo[0])
+        for now, later in zip(todo, todo[1:] + [None]):
+            if later is not None:
+                rotate(*later)
+            store(*now)
     else:
 
-        def one_source(source, carry):
-            rotate(source, 0)
-            store(source, 0)
-            return carry
-
-        lax.fori_loop(0, owners + 1, one_source, 0)
+        def one_source(distance, points):
+            rotate(distance, points, 0)
+            store(distance, points, 0)
+
+        each_source(owners, one_source)
 
     def out_copy(plane):
         return pltpu.make_async_copy(
             out_vmem.at[:, pl.ds(plane, 1)], out_ref.at[:, pl.ds(plane, 1)], out_sem.at[plane]
         )
 
+    def place(plane, block, variable, step=0):
+        return pl.ds(ROWS + (variable * planes + plane) * rows_count + block * ROWS + step, ROWS)
+
+    def flat(plane):
+        for block in range(blocks):
+            for variable in range(variables):
+                first = plane * plane_rows + block * ROWS * width + variable
+                plain[place(plane, block, variable), :] = table[pl.ds(first, ROWS, stride=width), :]
+
     def one_plane(plane):
         for block in range(blocks):
-            ratio = ratio_ref[plane, pl.ds(block * ROWS, ROWS), :]
-            inverse = 1.0 / (1.0 + 6.0 * ratio)
-            base = (plane + 1) * plane_rows + block * ROWS * width
-
-            def get(step, variable):
-                return table[pl.ds(base + step * width + variable, ROWS, stride=width), :]
-
-            fringe = get(0, variables) > 0.5
+            rows = pl.ds(block * ROWS, ROWS)
+            ratio, divisor = ratio_ref[plane, rows, :], inverse[plane, rows, :]
+            first = plane * plane_rows + block * ROWS * width + variables
+            fringe = table[pl.ds(first, ROWS, stride=width), :] > 0.5
             for variable in range(variables):
-                here = get(0, variable)
-                up, down = get(1, variable), get(-1, variable)
+                here = plain[place(plane, block, variable), :]
+                up = plain[place(plane, block, variable, 1), :]
+                down = plain[place(plane, block, variable, -1), :]
                 if block == 0:
                     down = jnp.where(sublane == 0, 0.0, down)
                 if block == blocks - 1:
                     up = jnp.where(sublane == ROWS - 1, 0.0, up)
                 right = jnp.where(lane == LANES - 1, 0.0, pltpu.roll(here, LANES - 1, 1))
                 left = jnp.where(lane == 0, 0.0, pltpu.roll(here, 1, 1))
-                total = get(rows_count, variable) + get(-rows_count, variable)
-                total = total + up + down + right + left
-                smooth = (here + ratio * total) * inverse
-                out_vmem[variable, plane, pl.ds(block * ROWS, ROWS), :] = jnp.where(
-                    fringe, here, smooth
-                )
+                if plane == 0:
+                    below = below_ref[variable, 0, rows, :]
+                else:
+                    below = plain[place(plane - 1, block, variable), :]
+                if plane == planes - 1:
+                    above = next_ref[3 + variable, 0, rows, :]
+                else:
+                    above = plain[place(plane + 1, block, variable), :]
+                total = (above + below) + (up + down) + (right + left)
+                smooth = (here + ratio * total) * divisor
+                out_vmem[variable, plane, rows, :] = jnp.where(fringe, here, smooth)
         out_copy(plane).start()
 
+    flat(0)
     for plane in range(planes):
+        if plane < planes - 1:
+            flat(plane + 1)
         one_plane(plane)
     for plane in range(planes):
         out_copy(plane).wait()
@@ -416,10 +438,12 @@
         out_specs=VMEM,
         scratch_shapes=[
             pltpu.VMEM(((planes + 1) * cols_count * 2, LANES), f32),
+            pltpu.VMEM((owners * 8, LANES), f32),
             pltpu.VMEM((owners + 8, LANES), i32),
             pltpu.SMEM((owners + 8, LANES), i32),
             pltpu.VMEM((8 * (owners + 1) * 8, LANES), f32),
             pltpu.VMEM((9, 8, ROWS, LANES), f32),
+            pltpu.VMEM((ROWS * 8, LANES), f32),
             pltpu.SemaphoreType.DMA,
         ],
         compiler_params=params,
@@ -433,9 +457,11 @@
         in_specs=[VMEM] * 6,
         out_specs=HBM,
         scratch_shapes=[
-            pltpu.VMEM(((planes + 2) * rows_count * 8 + 8, LANES), f32),
+            pltpu.VMEM((planes * rows_count * 8 + 8, LANES), f32),
             pltpu.SMEM(codes.shape, i32),
             pltpu.VMEM(((owners + 1 if owners <= 8 else 1) * LANES * ROWS, LANES), f32),
+            pltpu.VMEM((variables * planes * rows_count + 2 * ROWS, LANES), f32),
+            pltpu.VMEM(time_ratio.shape, f32),
             pltpu.VMEM(field.shape, f32),
             pltpu.SemaphoreType.DMA,
             pltpu.SemaphoreType.DMA((planes,)),

time: 32 us -> 31.5 us (0.984)
  Pallas kernels: 7.57 us -> 7.12 us
where the time goes in v4:
time: 31.5 us; the launch traced here: 31.3 us
  blocking collectives  21.7 us (69%)
  Pallas kernels  7.12 us (23%)
  starting transfers between devices  2.43 us (8%)
    all_to_all x1, blocking collectives, on_device(): lax.all_to_all(message, 'grid', split_axis=0, concat_axis=0, tiled=True)  12.3 us
    all_to_all x1, blocking collectives, on_device(): lax.all_to_all(values, 'grid', split_axis=0, concat_axis=0, tiled=True)  9.42 us
    pallas_call x1, Pallas kernels, on_device(): pl.pallas_call(functools.partial(relax_kernel, owners), out_shape=jax.Sha...  3.51 us
    pallas_call x1, Pallas kernels, on_device(): pl.pallas_call(functools.partial(gather_kernel, owners), out_shape=jax.Sh...  2.46 us
    ppermute x2, starting transfers between devices, passed_along(): return lax.ppermute(value, axis, pairs)  2.43 us
    pallas_call x1, Pallas kernels, on_device(): pl.pallas_call(first_kernel, out_shape=[jax.ShapeDtypeStruct((owners, 8,...  1.15 us
  transfers between devices with their start and end apart: 2, of which 0 were waited for; matrix products, arithmetic and copies ran while one was open for 0% of the time, Pallas kernels for 0%

profile of v4, /device:TPU:0, one launch (start us, length us, event | category | flops | bytes accessed | tf_op | source)
XLA Modules:
  0.0 31.3 jit_solution(10065958834449118604)
XLA Ops:
  0.0 0.0 copy-start
  0.0 0.0 copy-start.1
  0.0 1.1 %first.1 = (f32[8,8,128]{2,1,0:T(8,128)S(1)}, s32[24,128]{1,0:T(8,128)S(1)}, f32[8,1,32,128]{3,2,1,0:T(8,128)S(1)}, f32[5,1,32,128]{3,2,1,0:T(8,128)S(1)}) custom-call(s32[1,8]{1,0:T(1,128)} %count_ref.1, s32[1,8,2,128]{3,2,1,0:T(2,128)} %cell_ref.1, f32[1,8,3,2,128]{4,3,2,1,0:T(2,128)} %bitcast.7, s32[1,8,2,128]{3,2,1,0:T(2,128)} %node_ref.1, ...), custom_call_target="tpu_custom_call" | custom-call | tf_op jit(solution)/shard_map/first/pallas_call | solution.py:408
  1.2 2.4 %collective-permute-start = (f32[8,1,32,128]{3,2,1,0:T(8,128)S(1)}, f32[8,1,32,128]{3,2,1,0:T(8,128)S(1)}, u32[]{:S(2)}, u32[]{:S(2)}) collective-permute-start(f32[8,1,32,128]{3,2,1,0:T(8,128)S(1)} %get-tuple-element.10), channel_id=1, source_target_pairs={{0,3},{1,0},{2,1},{3,2},{4,7},{5,4},{6,5},{7,6},{8,11},{9,8},{10,9... | collective-permute-start | bytes 393224 | tf_op jit(solution)/shard_map/ppermute | solution.py:20
  3.6 0.0 collective-permute-start.1
  3.6 12.3 %all_to_all.10 = f32[8,8,128]{2,1,0:T(8,128)S(1)} all-to-all(f32[8,8,128]{2,1,0:T(8,128)S(1)} %get-tuple-element.12), channel_id=1, replica_groups=mesh['grid'=8,'sub'=4] {'grid'}, dimensions={0} | all-to-all | bytes 65536 | tf_op jit(solution)/shard_map/all_to_all | solution.py:433
  15.9 0.0 collective-permute-done.1.below_ref
  15.9 0.0 collective-permute-done.next_ref
  15.9 0.0 copy-done
  15.9 0.0 copy-done.1
  15.9 2.5 %gather.1 = f32[128,128]{1,0:T(8,128)S(1)} custom-call(f32[5,8,32,128]{3,2,1,0:T(8,128)S(1)} %copy-done, f32[3,8,32,128]{3,2,1,0:T(8,128)S(1)} %copy-done.1, f32[8,1,32,128]{3,2,1,0:T(8,128)S(1)} %collective-permute-done.next_ref, f32[5,1,32,128]{3,2,1,0:T(8,128)S(1)} %collective-permute-done.1.below_ref, f32[64,128]{1,0:T(8,128)S(1)} %bitcast.6), custom_call_target="tpu_custom_call" | custom-call | tf_op jit(solution)/shard_map/gather/pallas_call | solution.py:434
  18.4 0.0 copy-start.2
  18.4 9.4 %all_to_all.11 = f32[8,16,128]{2,1,0:T(8,128)S(1)} all-to-all(f32[8,16,128]{2,1,0:T(8,128)S(1)} %bitcast.5), channel_id=1, replica_groups=mesh['grid'=8,'sub'=4] {'grid'}, dimensions={0} | all-to-all | bytes 131072 | tf_op jit(solution)/shard_map/all_to_all | solution.py:453
  27.8 0.0 copy-done.2
  27.8 3.5 %relax.1 = f32[5,8,32,128]{3,2,1,0:T(8,128)} custom-call(s32[24,128]{1,0:T(8,128)S(1)} %get-tuple-element.9.code_ref, f32[5,8,32,128]{3,2,1,0:T(8,128)S(1)} %copy-done, f32[8,1,32,128]{3,2,1,0:T(8,128)S(1)} %collective-permute-done.next_ref, f32[5,1,32,128]{3,2,1,0:T(8,128)S(1)} %collective-permute-done.1.below_ref, f32[8,32,128]{2,1,0:T(8,128)S(1)} %copy-done.2, ...), custom_call_target="tpu_custom_call" | custom-call | tf_op jit(solution)/shard_map/relax/pallas_call | solution.py:454
Async XLA Ops:
  0.0 15.9 %copy-start = (f32[5,8,32,128]{3,2,1,0:T(8,128)S(1)}, f32[5,8,32,128]{3,2,1,0:T(8,128)}, u32[]{:S(2)}) copy-start(f32[5,8,32,128]{3,2,1,0:T(8,128)} %field_ref.5) | copy-start | bytes 1966084
  0.0 15.9 %copy-start.1 = (f32[3,8,32,128]{3,2,1,0:T(8,128)S(1)}, f32[3,8,32,128]{3,2,1,0:T(8,128)}, u32[]{:S(2)}) copy-start(f32[3,8,32,128]{3,2,1,0:T(8,128)} %jitter_ref.3) | copy-start | bytes 1179652
  1.2 14.7 %collective-permute-start = (f32[8,1,32,128]{3,2,1,0:T(8,128)S(1)}, f32[8,1,32,128]{3,2,1,0:T(8,128)S(1)}, u32[]{:S(2)}, u32[]{:S(2)}) collective-permute-start(f32[8,1,32,128]{3,2,1,0:T(8,128)S(1)} %get-tuple-element.10), channel_id=1, source_target_pairs={{0,3},{1,0},{2,1},{3,2},{4,7},{5,4},{6,5},{7,6},{8,11},{9,8},{10,9... | collective-permute-start | bytes 393224 | tf_op jit(solution)/shard_map/ppermute | solution.py:20
  3.6 12.3 %collective-permute-start.1 = (f32[5,1,32,128]{3,2,1,0:T(8,128)S(1)}, f32[5,1,32,128]{3,2,1,0:T(8,128)S(1)}, u32[]{:S(2)}, u32[]{:S(2)}) collective-permute-start(f32[5,1,32,128]{3,2,1,0:T(8,128)S(1)} %get-tuple-element.11), channel_id=1, source_target_pairs={{0,1},{1,2},{2,3},{3,0},{4,5},{5,6},{6,7},{7,4},{8,9},{9,10},{10,1... | collective-permute-start | bytes 245768 | tf_op jit(solution)/shard_map/ppermute | solution.py:20
  18.4 9.4 %copy-start.2 = (f32[8,32,128]{2,1,0:T(8,128)S(1)}, f32[8,32,128]{2,1,0:T(8,128)}, u32[]{:S(2)}) copy-start(f32[8,32,128]{2,1,0:T(8,128)} %ratio_ref.1) | copy-start | bytes 393220

commit v5 on v4

--- a/solution.py
+++ b/solution.py
@@ -142,17 +142,19 @@
 
 
 def separated(tiles, lane):
-    for bit, distance in ((0, 1), (1, 32), (2, 64)):
-        low = (lane & distance) == 0
-        result = list(tiles)
-        for a in range(8):
-            b = a | (1 << bit)
-            if a == b:
-                continue
-            result[a] = jnp.where(low, tiles[a], pltpu.roll(tiles[b], distance, 1))
-            result[b] = jnp.where(low, pltpu.roll(tiles[a], LANES - distance, 1), tiles[b])
-        tiles = result
-    return tiles
+    even = (lane & 1) == 0
+    result = [None] * 8
+    for a1 in range(2):
+        block = ((lane - a1) & 127) >> 5
+        held = [jnp.where(even, tiles[2 * h + a1], tiles[2 * h + 1 - a1]) for h in range(4)]
+        masks = [block == h for h in range(4)]
+        for w in range(4):
+            tile = held[3]
+            for h in range(3):
+                tile = jnp.where(masks[(h + w) & 3], held[h], tile)
+            distance = (LANES - 32 * w - a1) % LANES
+            result[2 * w + a1] = pltpu.roll(tile, distance, 1) if distance else tile
+    return result
 
 
 def tile_rows(tile):
@@ -193,7 +195,7 @@
     def decode(cells, place):
         cells = cells.astype(jnp.int32)
         row = (cells >> 12) * (2 * LANES) + (cells & 127) * 2
-        shift = ((lane & 30) - ((cells >> 7) & (rows_count - 1))) & 127
+        shift = (lane - ((cells >> 7) & (rows_count - 1))) & 127
         decoded[place, :] = row * LANES + shift
 
     def of_source(distance):
@@ -212,10 +214,12 @@
     copy.wait()
 
     low = sublane < 4
-    pairs = [(lane & 30) == 2 * k for k in range(16)]
-
-    def one_source(source, points):
-        for block in range((points + 31) // 32):
+    pairs = [((lane - k) & 31) >> 1 for k in range(2)]
+
+    def one_source(source, points, blocks=range(4)):
+        for block in blocks:
+            if block * 32 >= points:
+                continue
             held = [None, None]
             for k in range(min(32, points)):
                 code = codes[source, block * 32 + k]
@@ -227,11 +231,15 @@
                 )
                 tile = pltpu.roll(tile, code & 127, 1)
                 k2 = k & 1
-                held[k2] = tile if held[k2] is None else jnp.where(pairs[k >> 1], tile, held[k2])
+                held[k2] = tile if held[k2] is None else jnp.where(pairs[k2] == k >> 1, tile, held[k2])
             for k in range(min(2, points)):
                 picked[tile_rows((2 * block + k) * (owners + 1) + source), :] = held[k]
 
-    each_source(owners, one_source)
+    if owners <= 8:
+        for block in range(4):
+            each_source(owners, lambda source, points: one_source(source, points, [block]))
+    else:
+        each_source(owners, one_source)
 
     def one_block(block, last):
         for s in range(8):

time: 31.5 us -> 31.2 us (level)
  Pallas kernels: 7.12 us -> 6.8 us
    pallas_call x1, Pallas kernels: 2.46 us -> 2.14 us  [on_device(): pl.pallas_call(functools.partial(gather_kernel, owners), out_shape=jax.Sh...]
where the time goes in v5:
time: 31.2 us; the launch traced here: 31 us
  blocking collectives  21.7 us (70%)
  Pallas kernels  6.8 us (22%)
  starting transfers between devices  2.43 us (8%)
    all_to_all x1, blocking collectives, on_device(): lax.all_to_all(message, 'grid', split_axis=0, concat_axis=0, tiled=True)  12.3 us
    all_to_all x1, blocking collectives, on_device(): lax.all_to_all(values, 'grid', split_axis=0, concat_axis=0, tiled=True)  9.42 us
    pallas_call x1, Pallas kernels, on_device(): pl.pallas_call(functools.partial(relax_kernel, owners), out_shape=jax.Sha...  3.51 us
    ppermute x2, starting transfers between devices, passed_along(): return lax.ppermute(value, axis, pairs)  2.43 us
    pallas_call x1, Pallas kernels, on_device(): pl.pallas_call(functools.partial(gather_kernel, owners), out_shape=jax.Sh...  2.14 us
    pallas_call x1, Pallas kernels, on_device(): pl.pallas_call(first_kernel, out_shape=[jax.ShapeDtypeStruct((owners, 8,...  1.15 us
  transfers between devices with their start and end apart: 2, of which 0 were waited for; matrix products, arithmetic and copies ran while one was open for 0% of the time, Pallas kernels for 0%

profile of v5, /device:TPU:0, one launch (start us, length us, event | category | flops | bytes accessed | tf_op | source)
XLA Modules:
  0.0 31.0 jit_solution(4128462573488086121)
XLA Ops:
  0.0 0.0 copy-start
  0.0 0.0 copy-start.1
  0.0 1.1 %first.1 = (f32[8,8,128]{2,1,0:T(8,128)S(1)}, s32[24,128]{1,0:T(8,128)S(1)}, f32[8,1,32,128]{3,2,1,0:T(8,128)S(1)}, f32[5,1,32,128]{3,2,1,0:T(8,128)S(1)}) custom-call(s32[1,8]{1,0:T(1,128)} %count_ref.1, s32[1,8,2,128]{3,2,1,0:T(2,128)} %cell_ref.1, f32[1,8,3,2,128]{4,3,2,1,0:T(2,128)} %bitcast.7, s32[1,8,2,128]{3,2,1,0:T(2,128)} %node_ref.1, ...), custom_call_target="tpu_custom_call" | custom-call | tf_op jit(solution)/shard_map/first/pallas_call | solution.py:416
  1.2 2.4 %collective-permute-start = (f32[8,1,32,128]{3,2,1,0:T(8,128)S(1)}, f32[8,1,32,128]{3,2,1,0:T(8,128)S(1)}, u32[]{:S(2)}, u32[]{:S(2)}) collective-permute-start(f32[8,1,32,128]{3,2,1,0:T(8,128)S(1)} %get-tuple-element.10), channel_id=1, source_target_pairs={{0,3},{1,0},{2,1},{3,2},{4,7},{5,4},{6,5},{7,6},{8,11},{9,8},{10,9... | collective-permute-start | bytes 393224 | tf_op jit(solution)/shard_map/ppermute | solution.py:20
  3.6 0.0 collective-permute-start.1
  3.6 12.3 %all_to_all.10 = f32[8,8,128]{2,1,0:T(8,128)S(1)} all-to-all(f32[8,8,128]{2,1,0:T(8,128)S(1)} %get-tuple-element.12), channel_id=1, replica_groups=mesh['grid'=8,'sub'=4] {'grid'}, dimensions={0} | all-to-all | bytes 65536 | tf_op jit(solution)/shard_map/all_to_all | solution.py:441
  15.9 0.0 collective-permute-done.1.below_ref
  15.9 0.0 collective-permute-done.next_ref
  15.9 0.0 copy-done
  15.9 0.0 copy-done.1
  15.9 2.1 %gather.1 = f32[128,128]{1,0:T(8,128)S(1)} custom-call(f32[5,8,32,128]{3,2,1,0:T(8,128)S(1)} %copy-done, f32[3,8,32,128]{3,2,1,0:T(8,128)S(1)} %copy-done.1, f32[8,1,32,128]{3,2,1,0:T(8,128)S(1)} %collective-permute-done.next_ref, f32[5,1,32,128]{3,2,1,0:T(8,128)S(1)} %collective-permute-done.1.below_ref, f32[64,128]{1,0:T(8,128)S(1)} %bitcast.6), custom_call_target="tpu_custom_call" | custom-call | tf_op jit(solution)/shard_map/gather/pallas_call | solution.py:442
  18.1 0.0 copy-start.2
  18.1 9.4 %all_to_all.11 = f32[8,16,128]{2,1,0:T(8,128)S(1)} all-to-all(f32[8,16,128]{2,1,0:T(8,128)S(1)} %bitcast.5), channel_id=1, replica_groups=mesh['grid'=8,'sub'=4] {'grid'}, dimensions={0} | all-to-all | bytes 131072 | tf_op jit(solution)/shard_map/all_to_all | solution.py:461
  27.5 0.0 copy-done.2
  27.5 3.5 %relax.1 = f32[5,8,32,128]{3,2,1,0:T(8,128)} custom-call(s32[24,128]{1,0:T(8,128)S(1)} %get-tuple-element.9.code_ref, f32[5,8,32,128]{3,2,1,0:T(8,128)S(1)} %copy-done, f32[8,1,32,128]{3,2,1,0:T(8,128)S(1)} %collective-permute-done.next_ref, f32[5,1,32,128]{3,2,1,0:T(8,128)S(1)} %collective-permute-done.1.below_ref, f32[8,32,128]{2,1,0:T(8,128)S(1)} %copy-done.2, ...), custom_call_target="tpu_custom_call" | custom-call | tf_op jit(solution)/shard_map/relax/pallas_call | solution.py:462
Async XLA Ops:
  0.0 15.9 %copy-start = (f32[5,8,32,128]{3,2,1,0:T(8,128)S(1)}, f32[5,8,32,128]{3,2,1,0:T(8,128)}, u32[]{:S(2)}) copy-start(f32[5,8,32,128]{3,2,1,0:T(8,128)} %field_ref.5) | copy-start | bytes 1966084
  0.0 15.9 %copy-start.1 = (f32[3,8,32,128]{3,2,1,0:T(8,128)S(1)}, f32[3,8,32,128]{3,2,1,0:T(8,128)}, u32[]{:S(2)}) copy-start(f32[3,8,32,128]{3,2,1,0:T(8,128)} %jitter_ref.3) | copy-start | bytes 1179652
  1.2 14.7 %collective-permute-start = (f32[8,1,32,128]{3,2,1,0:T(8,128)S(1)}, f32[8,1,32,128]{3,2,1,0:T(8,128)S(1)}, u32[]{:S(2)}, u32[]{:S(2)}) collective-permute-start(f32[8,1,32,128]{3,2,1,0:T(8,128)S(1)} %get-tuple-element.10), channel_id=1, source_target_pairs={{0,3},{1,0},{2,1},{3,2},{4,7},{5,4},{6,5},{7,6},{8,11},{9,8},{10,9... | collective-permute-start | bytes 393224 | tf_op jit(solution)/shard_map/ppermute | solution.py:20
  3.6 12.3 %collective-permute-start.1 = (f32[5,1,32,128]{3,2,1,0:T(8,128)S(1)}, f32[5,1,32,128]{3,2,1,0:T(8,128)S(1)}, u32[]{:S(2)}, u32[]{:S(2)}) collective-permute-start(f32[5,1,32,128]{3,2,1,0:T(8,128)S(1)} %get-tuple-element.11), channel_id=1, source_target_pairs={{0,1},{1,2},{2,3},{3,0},{4,5},{5,6},{6,7},{7,4},{8,9},{9,10},{10,1... | collective-permute-start | bytes 245768 | tf_op jit(solution)/shard_map/ppermute | solution.py:20
  18.1 9.4 %copy-start.2 = (f32[8,32,128]{2,1,0:T(8,128)S(1)}, f32[8,32,128]{2,1,0:T(8,128)}, u32[]{:S(2)}) copy-start(f32[8,32,128]{2,1,0:T(8,128)} %ratio_ref.1) | copy-start | bytes 393220

commit v6 on v5

--- a/solution.py
+++ b/solution.py
@@ -12,6 +12,7 @@
 VMEM = pl.BlockSpec(memory_space=pltpu.VMEM)
 HBM = pl.BlockSpec(memory_space=pltpu.HBM)
 LIMIT = 24 << 20
+EARLY = (0, 1, )
 
 
 def passed_along(value, axis, steps):
@@ -308,10 +309,9 @@
                 table[pl.ds(first, rows_count, stride=width), :] = tile
             inverse[plane] = 1.0 / (1.0 + 6.0 * ratio_ref[plane])
 
-    after(me, lay_out_rows)
-    copy.wait()
-
-    def rotate(distance, points, buffer):
+    lane_id = lane.astype(jnp.float32)
+
+    def values_of(distance):
         if isinstance(distance, int):
             owner = lax.rem(me + distance % owners + distance // owners, owners)
             first = owner * 16 + 8 * (distance // owners)
@@ -320,7 +320,20 @@
             owner = lax.rem(jnp.where(more, me + 1, me + distance), owners)
             first = owner * 16 + jnp.where(more, 8, 0)
         tile = values_ref[pl.ds(pl.multiple_of(first, 8), 8), :]
-        tile = jnp.where(sublane == variables, 1.0, tile)
+        return jnp.where(sublane == variables, 1.0, tile)
+
+    def spread(distance, points, buffer):
+        column = (code_ref[pl.ds(owners + 1 + distance, 1), :] + lane[:1]) & (LANES - 1)
+        tile = jnp.where(
+            sublane == variables + 1, column.astype(jnp.float32), values_of(distance)
+        )
+        for point in range(points):
+            rolled[tile_rows(buffer * LANES + point), :] = jnp.broadcast_to(
+                tile[:, point : point + 1], (ROWS, LANES)
+            )
+
+    def rotate(distance, points, buffer):
+        tile = values_of(distance)
         tile = jnp.where(sublane == variables + 1, lane.astype(jnp.float32), tile)
         for point in range(points):
             place = tile_rows(buffer * LANES + point)
@@ -331,21 +344,37 @@
             place = (buffer * LANES + point) * ROWS
             tag = rolled[place + variables + 1 : place + variables + 2, :]
             row = pl.multiple_of(codes[distance, point], width)
+            tag = jnp.broadcast_to(tag, (ROWS, LANES))
+            early = isinstance(distance, int) and distance in EARLY
             pltpu.store(
                 table.at[pl.ds(row, width), :],
                 rolled[place : place + ROWS, :],
-                mask=jnp.broadcast_to(tag, (ROWS, LANES)) == float(point),
+                mask=tag == (lane_id if early else float(point)),
             )
 
     if owners <= 8:
         todo = []
         each_source(owners, lambda distance, points: todo.append((distance, points, distance)))
-        rotate(*todo[0])
-        for now, later in zip(todo, todo[1:] + [None]):
+
+        def meanwhile():
+            lay_out_rows()
+            for distance in EARLY:
+                spread(distance, LANES, distance)
+
+        after(me, meanwhile)
+        copy.wait()
+        late = [item for item in todo if item[0] not in EARLY]
+        rotate(*late[0])
+        for distance in EARLY:
+            store(distance, LANES, distance)
+        for now, later in zip(late, late[1:] + [None]):
             if later is not None:
                 rotate(*later)
             store(*now)
     else:
+
+        after(me, lay_out_rows)
+        copy.wait()
 
         def one_source(distance, points):
             rotate(distance, points, 0)

time: 31.2 us -> 30.9 us (level)
  Pallas kernels: 6.8 us -> 6.47 us
    pallas_call x1, Pallas kernels: 3.51 us -> 3.18 us  [on_device(): pl.pallas_call(functools.partial(relax_kernel, owners), out_shape=jax.Sha...]
where the time goes in v6:
time: 30.9 us; the launch traced here: 30.7 us
  blocking collectives  21.7 us (70%)
  Pallas kernels  6.47 us (21%)
  starting transfers between devices  2.43 us (8%)
    all_to_all x1, blocking collectives, on_device(): lax.all_to_all(message, 'grid', split_axis=0, concat_axis=0, tiled=True)  12.3 us
    all_to_all x1, blocking collectives, on_device(): lax.all_to_all(values, 'grid', split_axis=0, concat_axis=0, tiled=True)  9.42 us
    pallas_call x1, Pallas kernels, on_device(): pl.pallas_call(functools.partial(relax_kernel, owners), out_shape=jax.Sha...  3.18 us
    ppermute x2, starting transfers between devices, passed_along(): return lax.ppermute(value, axis, pairs)  2.43 us
    pallas_call x1, Pallas kernels, on_device(): pl.pallas_call(functools.partial(gather_kernel, owners), out_shape=jax.Sh...  2.14 us
    pallas_call x1, Pallas kernels, on_device(): pl.pallas_call(first_kernel, out_shape=[jax.ShapeDtypeStruct((owners, 8,...  1.15 us
  transfers between devices with their start and end apart: 2, of which 0 were waited for; matrix products, arithmetic and copies ran while one was open for 0% of the time, Pallas kernels for 0%

profile of v6, /device:TPU:0, one launch (start us, length us, event | category | flops | bytes accessed | tf_op | source)
XLA Modules:
  0.0 30.7 jit_solution(5051105827736526381)
XLA Ops:
  0.0 0.0 copy-start
  0.0 0.0 copy-start.1
  0.0 1.1 %first.1 = (f32[8,8,128]{2,1,0:T(8,128)S(1)}, s32[24,128]{1,0:T(8,128)S(1)}, f32[8,1,32,128]{3,2,1,0:T(8,128)S(1)}, f32[5,1,32,128]{3,2,1,0:T(8,128)S(1)}) custom-call(s32[1,8]{1,0:T(1,128)} %count_ref.1, s32[1,8,2,128]{3,2,1,0:T(2,128)} %cell_ref.1, f32[1,8,3,2,128]{4,3,2,1,0:T(2,128)} %bitcast.7, s32[1,8,2,128]{3,2,1,0:T(2,128)} %node_ref.1, ...), custom_call_target="tpu_custom_call" | custom-call | tf_op jit(solution)/shard_map/first/pallas_call | solution.py:445
  1.2 2.4 %collective-permute-start = (f32[8,1,32,128]{3,2,1,0:T(8,128)S(1)}, f32[8,1,32,128]{3,2,1,0:T(8,128)S(1)}, u32[]{:S(2)}, u32[]{:S(2)}) collective-permute-start(f32[8,1,32,128]{3,2,1,0:T(8,128)S(1)} %get-tuple-element.10), channel_id=1, source_target_pairs={{0,3},{1,0},{2,1},{3,2},{4,7},{5,4},{6,5},{7,6},{8,11},{9,8},{10,9... | collective-permute-start | bytes 393224 | tf_op jit(solution)/shard_map/ppermute | solution.py:21
  3.6 0.0 collective-permute-start.1
  3.6 12.3 %all_to_all.10 = f32[8,8,128]{2,1,0:T(8,128)S(1)} all-to-all(f32[8,8,128]{2,1,0:T(8,128)S(1)} %get-tuple-element.12), channel_id=1, replica_groups=mesh['grid'=8,'sub'=4] {'grid'}, dimensions={0} | all-to-all | bytes 65536 | tf_op jit(solution)/shard_map/all_to_all | solution.py:470
  15.9 0.0 collective-permute-done.1.below_ref
  15.9 0.0 collective-permute-done.next_ref
  15.9 0.0 copy-done
  15.9 0.0 copy-done.1
  15.9 2.1 %gather.1 = f32[128,128]{1,0:T(8,128)S(1)} custom-call(f32[5,8,32,128]{3,2,1,0:T(8,128)S(1)} %copy-done, f32[3,8,32,128]{3,2,1,0:T(8,128)S(1)} %copy-done.1, f32[8,1,32,128]{3,2,1,0:T(8,128)S(1)} %collective-permute-done.next_ref, f32[5,1,32,128]{3,2,1,0:T(8,128)S(1)} %collective-permute-done.1.below_ref, f32[64,128]{1,0:T(8,128)S(1)} %bitcast.6), custom_call_target="tpu_custom_call" | custom-call | tf_op jit(solution)/shard_map/gather/pallas_call | solution.py:471
  18.1 0.0 copy-start.2
  18.1 9.4 %all_to_all.11 = f32[8,16,128]{2,1,0:T(8,128)S(1)} all-to-all(f32[8,16,128]{2,1,0:T(8,128)S(1)} %bitcast.5), channel_id=1, replica_groups=mesh['grid'=8,'sub'=4] {'grid'}, dimensions={0} | all-to-all | bytes 131072 | tf_op jit(solution)/shard_map/all_to_all | solution.py:490
  27.5 0.0 copy-done.2
  27.5 3.2 %relax.1 = f32[5,8,32,128]{3,2,1,0:T(8,128)} custom-call(s32[24,128]{1,0:T(8,128)S(1)} %get-tuple-element.9.code_ref, f32[5,8,32,128]{3,2,1,0:T(8,128)S(1)} %copy-done, f32[8,1,32,128]{3,2,1,0:T(8,128)S(1)} %collective-permute-done.next_ref, f32[5,1,32,128]{3,2,1,0:T(8,128)S(1)} %collective-permute-done.1.below_ref, f32[8,32,128]{2,1,0:T(8,128)S(1)} %copy-done.2, ...), custom_call_target="tpu_custom_call" | custom-call | tf_op jit(solution)/shard_map/relax/pallas_call | solution.py:491
Async XLA Ops:
  0.0 15.9 %copy-start = (f32[5,8,32,128]{3,2,1,0:T(8,128)S(1)}, f32[5,8,32,128]{3,2,1,0:T(8,128)}, u32[]{:S(2)}) copy-start(f32[5,8,32,128]{3,2,1,0:T(8,128)} %field_ref.5) | copy-start | bytes 1966084
  0.0 15.9 %copy-start.1 = (f32[3,8,32,128]{3,2,1,0:T(8,128)S(1)}, f32[3,8,32,128]{3,2,1,0:T(8,128)}, u32[]{:S(2)}) copy-start(f32[3,8,32,128]{3,2,1,0:T(8,128)} %jitter_ref.3) | copy-start | bytes 1179652
  1.2 14.7 %collective-permute-start = (f32[8,1,32,128]{3,2,1,0:T(8,128)S(1)}, f32[8,1,32,128]{3,2,1,0:T(8,128)S(1)}, u32[]{:S(2)}, u32[]{:S(2)}) collective-permute-start(f32[8,1,32,128]{3,2,1,0:T(8,128)S(1)} %get-tuple-element.10), channel_id=1, source_target_pairs={{0,3},{1,0},{2,1},{3,2},{4,7},{5,4},{6,5},{7,6},{8,11},{9,8},{10,9... | collective-permute-start | bytes 393224 | tf_op jit(solution)/shard_map/ppermute | solution.py:21
  3.6 12.3 %collective-permute-start.1 = (f32[5,1,32,128]{3,2,1,0:T(8,128)S(1)}, f32[5,1,32,128]{3,2,1,0:T(8,128)S(1)}, u32[]{:S(2)}, u32[]{:S(2)}) collective-permute-start(f32[5,1,32,128]{3,2,1,0:T(8,128)S(1)} %get-tuple-element.11), channel_id=1, source_target_pairs={{0,1},{1,2},{2,3},{3,0},{4,5},{5,6},{6,7},{7,4},{8,9},{9,10},{10,1... | collective-permute-start | bytes 245768 | tf_op jit(solution)/shard_map/ppermute | solution.py:21
  18.1 9.4 %copy-start.2 = (f32[8,32,128]{2,1,0:T(8,128)S(1)}, f32[8,32,128]{2,1,0:T(8,128)}, u32[]{:S(2)}) copy-start(f32[8,32,128]{2,1,0:T(8,128)} %ratio_ref.1) | copy-start | bytes 393220

commit v7 on v6

--- a/solution.py
+++ b/solution.py
@@ -12,7 +12,7 @@
 VMEM = pl.BlockSpec(memory_space=pltpu.VMEM)
 HBM = pl.BlockSpec(memory_space=pltpu.HBM)
 LIMIT = 24 << 20
-EARLY = (0, 1, )
+EARLY = (0, 1, 3,)
 
 
 def passed_along(value, axis, steps):
@@ -32,19 +32,19 @@
         pltpu.make_async_copy(source, target, sem.at[k])
         for k, (source, target) in enumerate(
             (
+                (jitter_ref.at[:, pl.ds(0, 1)], next_ref.at[pl.ds(0, 3)]),
+                (field_ref.at[:, pl.ds(0, 1)], next_ref.at[pl.ds(3, variables)]),
+                (field_ref.at[:, pl.ds(planes - 1, 1)], last_ref),
                 (count_ref, count_smem),
                 (cell_ref, cell_vmem),
                 (offset_ref, offset_vmem),
                 (node_ref, node_vmem),
-                (jitter_ref.at[:, pl.ds(0, 1)], next_ref.at[pl.ds(0, 3)]),
-                (field_ref.at[:, pl.ds(0, 1)], next_ref.at[pl.ds(3, variables)]),
-                (field_ref.at[:, pl.ds(planes - 1, 1)], last_ref),
             )
         )
     ]
     for copy in copies:
         copy.start()
-    for copy in copies[:4]:
+    for copy in copies[3:]:
         copy.wait()
 
     spare = planes * rows_count * 8
@@ -71,7 +71,7 @@
     lax.fori_loop(0, owners, one, 0, unroll=True)
     heavy = lax.rem(me + 1, owners)
     code(owners, node_vmem[0, heavy, 1:2, :], lane + points < count_smem[0, heavy])
-    for copy in copies[4:]:
+    for copy in copies[:3]:
         copy.wait()
 
 
@@ -209,7 +209,8 @@
         decode(cells, pl.ds(block * ROWS, ROWS))
     more = jnp.broadcast_to(message[12:13, :], (ROWS, LANES))
     decode(more, pl.ds(owners, ROWS))
-    copy = pltpu.make_async_copy(decoded, codes, sem)
+    needed = pl.ds(0, owners + 1)
+    copy = pltpu.make_async_copy(decoded.at[needed], codes.at[needed], sem)
     copy.start()
     after(me, lambda: lay_out(table, field_ref, jitter_ref, next_ref))
     copy.wait()
@@ -293,7 +294,8 @@
     width = 8
     blocks = rows_count // ROWS
     plane_rows = rows_count * width
-    copy = pltpu.make_async_copy(code_ref, codes, sem)
+    needed = pl.ds(0, 2 * owners + 2)
+    copy = pltpu.make_async_copy(code_ref.at[needed], codes.at[needed], sem)
     copy.start()
     lane = lax.broadcasted_iota(jnp.int32, (ROWS, LANES), 1)
     sublane = lax.broadcasted_iota(jnp.int32, (ROWS, LANES), 0)
@@ -322,15 +324,17 @@
         tile = values_ref[pl.ds(pl.multiple_of(first, 8), 8), :]
         return jnp.where(sublane == variables, 1.0, tile)
 
-    def spread(distance, points, buffer):
-        column = (code_ref[pl.ds(owners + 1 + distance, 1), :] + lane[:1]) & (LANES - 1)
-        tile = jnp.where(
-            sublane == variables + 1, column.astype(jnp.float32), values_of(distance)
-        )
-        for point in range(points):
-            rolled[tile_rows(buffer * LANES + point), :] = jnp.broadcast_to(
-                tile[:, point : point + 1], (ROWS, LANES)
-            )
+    def spread(distances):
+        tiles = []
+        for distance in distances:
+            column = (code_ref[pl.ds(owners + 1 + distance, 1), :] + lane[:1]) & (LANES - 1)
+            column = column.astype(jnp.float32)
+            tiles.append(jnp.where(sublane == variables + 1, column, values_of(distance)))
+        for point in range(LANES):
+            for distance, tile in zip(distances, tiles):
+                rolled[tile_rows(distance * LANES + point), :] = jnp.broadcast_to(
+                    tile[:, point : point + 1], (ROWS, LANES)
+                )
 
     def rotate(distance, points, buffer):
         tile = values_of(distance)
@@ -358,8 +362,7 @@
 
         def meanwhile():
             lay_out_rows()
-            for distance in EARLY:
-                spread(distance, LANES, distance)
+            spread(EARLY)
 
         after(me, meanwhile)
         copy.wait()

time: 30.9 us -> 30.7 us (level)
  no operation moved by 1% of the time
where the time goes in v7:
time: 30.7 us; the launch traced here: 30.5 us
  blocking collectives  21.7 us (71%)
  Pallas kernels  6.25 us (20%)
  starting transfers between devices  2.43 us (8%)
    all_to_all x1, blocking collectives, on_device(): lax.all_to_all(message, 'grid', split_axis=0, concat_axis=0, tiled=True)  12.3 us
    all_to_all x1, blocking collectives, on_device(): lax.all_to_all(values, 'grid', split_axis=0, concat_axis=0, tiled=True)  9.42 us
    pallas_call x1, Pallas kernels, on_device(): pl.pallas_call(functools.partial(relax_kernel, owners), out_shape=jax.Sha...  3.07 us
    ppermute x2, starting transfers between devices, passed_along(): return lax.ppermute(value, axis, pairs)  2.43 us
    pallas_call x1, Pallas kernels, on_device(): pl.pallas_call(functools.partial(gather_kernel, owners), out_shape=jax.Sh...  2.08 us
    pallas_call x1, Pallas kernels, on_device(): pl.pallas_call(first_kernel, out_shape=[jax.ShapeDtypeStruct((owners, 8,...  1.1 us
  transfers between devices with their start and end apart: 2, of which 0 were waited for; matrix products, arithmetic and copies ran while one was open for 0% of the time, Pallas kernels for 0%

profile of v7, /device:TPU:0, one launch (start us, length us, event | category | flops | bytes accessed | tf_op | source)
XLA Modules:
  0.0 30.5 jit_solution(8200875285786712783)
XLA Ops:
  0.0 0.0 copy-start
  0.0 0.0 copy-start.1
  0.0 1.1 %first.1 = (f32[8,8,128]{2,1,0:T(8,128)S(1)}, s32[24,128]{1,0:T(8,128)S(1)}, f32[8,1,32,128]{3,2,1,0:T(8,128)S(1)}, f32[5,1,32,128]{3,2,1,0:T(8,128)S(1)}) custom-call(s32[1,8]{1,0:T(1,128)} %count_ref.1, s32[1,8,2,128]{3,2,1,0:T(2,128)} %cell_ref.1, f32[1,8,3,2,128]{4,3,2,1,0:T(2,128)} %bitcast.7, s32[1,8,2,128]{3,2,1,0:T(2,128)} %node_ref.1, ...), custom_call_target="tpu_custom_call" | custom-call | tf_op jit(solution)/shard_map/first/pallas_call | solution.py:448
  1.1 2.4 %collective-permute-start = (f32[8,1,32,128]{3,2,1,0:T(8,128)S(1)}, f32[8,1,32,128]{3,2,1,0:T(8,128)S(1)}, u32[]{:S(2)}, u32[]{:S(2)}) collective-permute-start(f32[8,1,32,128]{3,2,1,0:T(8,128)S(1)} %get-tuple-element.10), channel_id=1, source_target_pairs={{0,3},{1,0},{2,1},{3,2},{4,7},{5,4},{6,5},{7,6},{8,11},{9,8},{10,9... | collective-permute-start | bytes 393224 | tf_op jit(solution)/shard_map/ppermute | solution.py:21
  3.5 0.0 collective-permute-start.1
  3.5 12.3 %all_to_all.10 = f32[8,8,128]{2,1,0:T(8,128)S(1)} all-to-all(f32[8,8,128]{2,1,0:T(8,128)S(1)} %get-tuple-element.12), channel_id=1, replica_groups=mesh['grid'=8,'sub'=4] {'grid'}, dimensions={0} | all-to-all | bytes 65536 | tf_op jit(solution)/shard_map/all_to_all | solution.py:473
  15.9 0.0 collective-permute-done.1.below_ref
  15.9 0.0 collective-permute-done.next_ref
  15.9 0.0 copy-done
  15.9 0.0 copy-done.1
  15.9 2.1 %gather.1 = f32[128,128]{1,0:T(8,128)S(1)} custom-call(f32[5,8,32,128]{3,2,1,0:T(8,128)S(1)} %copy-done, f32[3,8,32,128]{3,2,1,0:T(8,128)S(1)} %copy-done.1, f32[8,1,32,128]{3,2,1,0:T(8,128)S(1)} %collective-permute-done.next_ref, f32[5,1,32,128]{3,2,1,0:T(8,128)S(1)} %collective-permute-done.1.below_ref, f32[64,128]{1,0:T(8,128)S(1)} %bitcast.6), custom_call_target="tpu_custom_call" | custom-call | tf_op jit(solution)/shard_map/gather/pallas_call | solution.py:474
  18.0 0.0 copy-start.2
  18.0 9.4 %all_to_all.11 = f32[8,16,128]{2,1,0:T(8,128)S(1)} all-to-all(f32[8,16,128]{2,1,0:T(8,128)S(1)} %bitcast.5), channel_id=1, replica_groups=mesh['grid'=8,'sub'=4] {'grid'}, dimensions={0} | all-to-all | bytes 131072 | tf_op jit(solution)/shard_map/all_to_all | solution.py:493
  27.4 0.0 copy-done.2
  27.4 3.1 %relax.1 = f32[5,8,32,128]{3,2,1,0:T(8,128)} custom-call(s32[24,128]{1,0:T(8,128)S(1)} %get-tuple-element.9.code_ref, f32[5,8,32,128]{3,2,1,0:T(8,128)S(1)} %copy-done, f32[8,1,32,128]{3,2,1,0:T(8,128)S(1)} %collective-permute-done.next_ref, f32[5,1,32,128]{3,2,1,0:T(8,128)S(1)} %collective-permute-done.1.below_ref, f32[8,32,128]{2,1,0:T(8,128)S(1)} %copy-done.2, ...), custom_call_target="tpu_custom_call" | custom-call | tf_op jit(solution)/shard_map/relax/pallas_call | solution.py:494
Async XLA Ops:
  0.0 15.9 %copy-start = (f32[5,8,32,128]{3,2,1,0:T(8,128)S(1)}, f32[5,8,32,128]{3,2,1,0:T(8,128)}, u32[]{:S(2)}) copy-start(f32[5,8,32,128]{3,2,1,0:T(8,128)} %field_ref.5) | copy-start | bytes 1966084
  0.0 15.9 %copy-start.1 = (f32[3,8,32,128]{3,2,1,0:T(8,128)S(1)}, f32[3,8,32,128]{3,2,1,0:T(8,128)}, u32[]{:S(2)}) copy-start(f32[3,8,32,128]{3,2,1,0:T(8,128)} %jitter_ref.3) | copy-start | bytes 1179652
  1.1 14.7 %collective-permute-start = (f32[8,1,32,128]{3,2,1,0:T(8,128)S(1)}, f32[8,1,32,128]{3,2,1,0:T(8,128)S(1)}, u32[]{:S(2)}, u32[]{:S(2)}) collective-permute-start(f32[8,1,32,128]{3,2,1,0:T(8,128)S(1)} %get-tuple-element.10), channel_id=1, source_target_pairs={{0,3},{1,0},{2,1},{3,2},{4,7},{5,4},{6,5},{7,6},{8,11},{9,8},{10,9... | collective-permute-start | bytes 393224 | tf_op jit(solution)/shard_map/ppermute | solution.py:21
  3.5 12.3 %collective-permute-start.1 = (f32[5,1,32,128]{3,2,1,0:T(8,128)S(1)}, f32[5,1,32,128]{3,2,1,0:T(8,128)S(1)}, u32[]{:S(2)}, u32[]{:S(2)}) collective-permute-start(f32[5,1,32,128]{3,2,1,0:T(8,128)S(1)} %get-tuple-element.11), channel_id=1, source_target_pairs={{0,1},{1,2},{2,3},{3,0},{4,5},{5,6},{6,7},{7,4},{8,9},{9,10},{10,1... | collective-permute-start | bytes 245768 | tf_op jit(solution)/shard_map/ppermute | solution.py:21
  18.0 9.4 %copy-start.2 = (f32[8,32,128]{2,1,0:T(8,128)S(1)}, f32[8,32,128]{2,1,0:T(8,128)}, u32[]{:S(2)}) copy-start(f32[8,32,128]{2,1,0:T(8,128)} %ratio_ref.1) | copy-start | bytes 393220

commit v8 on v7

--- a/solution.py
+++ b/solution.py
@@ -61,7 +61,8 @@
         count = count_smem[0, owner]
         cells = cell_vmem[0, owner].astype(jnp.float32)
         message_ref[owner, 0:1, :] = cells[0:1]
-        message_ref[owner, 4:5, :] = cells[1:2]
+        counts = jnp.full((1, points), count, jnp.int32).astype(jnp.float32)
+        message_ref[owner, 4:5, :] = jnp.where(distance == 1, cells[1:2], counts)
         for c in range(3):
             message_ref[owner, 1 + c : 2 + c, :] = offset_vmem[0, owner, c, 0:1, :]
             message_ref[owner, 5 + c : 6 + c, :] = offset_vmem[0, owner, c, 1:2, :]
@@ -209,7 +210,10 @@
         decode(cells, pl.ds(block * ROWS, ROWS))
     more = jnp.broadcast_to(message[12:13, :], (ROWS, LANES))
     decode(more, pl.ds(owners, ROWS))
-    needed = pl.ds(0, owners + 1)
+    most = jnp.where(sublane == 1, 0.0, message[pl.ds(4, ROWS, stride=8), :])
+    most = jnp.max(most, axis=0, keepdims=True).astype(jnp.int32)
+    decoded[owners + 1 : owners + 2, :] = most
+    needed = pl.ds(0, owners + 2)
     copy = pltpu.make_async_copy(decoded.at[needed], codes.at[needed], sem)
     copy.start()
     after(me, lambda: lay_out(table, field_ref, jitter_ref, next_ref))
@@ -238,8 +242,20 @@
                 picked[tile_rows((2 * block + k) * (owners + 1) + source), :] = held[k]
 
     if owners <= 8:
-        for block in range(4):
-            each_source(owners, lambda source, points: one_source(source, points, [block]))
+        def blocks_of(sources, blocks):
+            for block in blocks:
+                for source in sources:
+                    one_source(source, 1 if source == 2 else LANES, [block])
+
+        full = [1, owners]
+        others = [source for source in range(owners) if source not in full]
+
+        @pl.when(codes[owners + 1, 0] > LANES // 2)
+        def _():
+            blocks_of(others, (2, 3))
+
+        blocks_of(others + full, (0, 1))
+        blocks_of(full, (2, 3))
     else:
         each_source(owners, one_source)
 

time: 30.7 us -> 30.6 us (level)
  Pallas kernels: 6.25 us -> 5.86 us
    pallas_call x1, Pallas kernels: 2.08 us -> 1.7 us  [on_device(): pl.pallas_call(functools.partial(gather_kernel, owners), out_shape=jax.Sh...]
where the time goes in v8:
time: 30.6 us; the launch traced here: 30.1 us
  blocking collectives  21.7 us (71%)
  Pallas kernels  5.86 us (19%)
  starting transfers between devices  2.43 us (8%)
    all_to_all x1, blocking collectives, on_device(): lax.all_to_all(message, 'grid', split_axis=0, concat_axis=0, tiled=True)  12.3 us
    all_to_all x1, blocking collectives, on_device(): lax.all_to_all(values, 'grid', split_axis=0, concat_axis=0, tiled=True)  9.42 us
    pallas_call x1, Pallas kernels, on_device(): pl.pallas_call(functools.partial(relax_kernel, owners), out_shape=jax.Sha...  3.06 us
    ppermute x2, starting transfers between devices, passed_along(): return lax.ppermute(value, axis, pairs)  2.43 us
    pallas_call x1, Pallas kernels, on_device(): pl.pallas_call(functools.partial(gather_kernel, owners), out_shape=jax.Sh...  1.7 us
    pallas_call x1, Pallas kernels, on_device(): pl.pallas_call(first_kernel, out_shape=[jax.ShapeDtypeStruct((owners, 8,...  1.1 us
  transfers between devices with their start and end apart: 2, of which 0 were waited for; matrix products, arithmetic and copies ran while one was open for 0% of the time, Pallas kernels for 0%

profile of v8, /device:TPU:0, one launch (start us, length us, event | category | flops | bytes accessed | tf_op | source)
XLA Modules:
  0.0 30.1 jit_solution(11938072921495078366)
XLA Ops:
  0.0 0.0 copy-start
  0.0 0.0 copy-start.1
  0.0 1.1 %first.1 = (f32[8,8,128]{2,1,0:T(8,128)S(1)}, s32[24,128]{1,0:T(8,128)S(1)}, f32[8,1,32,128]{3,2,1,0:T(8,128)S(1)}, f32[5,1,32,128]{3,2,1,0:T(8,128)S(1)}) custom-call(s32[1,8]{1,0:T(1,128)} %count_ref.1, s32[1,8,2,128]{3,2,1,0:T(2,128)} %cell_ref.1, f32[1,8,3,2,128]{4,3,2,1,0:T(2,128)} %bitcast.7, s32[1,8,2,128]{3,2,1,0:T(2,128)} %node_ref.1, ...), custom_call_target="tpu_custom_call" | custom-call | tf_op jit(solution)/shard_map/first/pallas_call | solution.py:464
  1.1 2.4 %collective-permute-start = (f32[8,1,32,128]{3,2,1,0:T(8,128)S(1)}, f32[8,1,32,128]{3,2,1,0:T(8,128)S(1)}, u32[]{:S(2)}, u32[]{:S(2)}) collective-permute-start(f32[8,1,32,128]{3,2,1,0:T(8,128)S(1)} %get-tuple-element.10), channel_id=1, source_target_pairs={{0,3},{1,0},{2,1},{3,2},{4,7},{5,4},{6,5},{7,6},{8,11},{9,8},{10,9... | collective-permute-start | bytes 393224 | tf_op jit(solution)/shard_map/ppermute | solution.py:21
  3.5 0.0 collective-permute-start.1
  3.5 12.3 %all_to_all.10 = f32[8,8,128]{2,1,0:T(8,128)S(1)} all-to-all(f32[8,8,128]{2,1,0:T(8,128)S(1)} %get-tuple-element.12), channel_id=1, replica_groups=mesh['grid'=8,'sub'=4] {'grid'}, dimensions={0} | all-to-all | bytes 65536 | tf_op jit(solution)/shard_map/all_to_all | solution.py:489
  15.9 0.0 collective-permute-done.1.below_ref
  15.9 0.0 collective-permute-done.next_ref
  15.9 0.0 copy-done
  15.9 0.0 copy-done.1
  15.9 1.7 %gather.1 = f32[128,128]{1,0:T(8,128)S(1)} custom-call(f32[5,8,32,128]{3,2,1,0:T(8,128)S(1)} %copy-done, f32[3,8,32,128]{3,2,1,0:T(8,128)S(1)} %copy-done.1, f32[8,1,32,128]{3,2,1,0:T(8,128)S(1)} %collective-permute-done.next_ref, f32[5,1,32,128]{3,2,1,0:T(8,128)S(1)} %collective-permute-done.1.below_ref, f32[64,128]{1,0:T(8,128)S(1)} %bitcast.6), custom_call_target="tpu_custom_call" | custom-call | tf_op jit(solution)/shard_map/gather/pallas_call | solution.py:490
  17.6 0.0 copy-start.2
  17.6 9.4 %all_to_all.11 = f32[8,16,128]{2,1,0:T(8,128)S(1)} all-to-all(f32[8,16,128]{2,1,0:T(8,128)S(1)} %bitcast.5), channel_id=1, replica_groups=mesh['grid'=8,'sub'=4] {'grid'}, dimensions={0} | all-to-all | bytes 131072 | tf_op jit(solution)/shard_map/all_to_all | solution.py:509
  27.0 0.0 copy-done.2
  27.0 3.1 %relax.1 = f32[5,8,32,128]{3,2,1,0:T(8,128)} custom-call(s32[24,128]{1,0:T(8,128)S(1)} %get-tuple-element.9.code_ref, f32[5,8,32,128]{3,2,1,0:T(8,128)S(1)} %copy-done, f32[8,1,32,128]{3,2,1,0:T(8,128)S(1)} %collective-permute-done.next_ref, f32[5,1,32,128]{3,2,1,0:T(8,128)S(1)} %collective-permute-done.1.below_ref, f32[8,32,128]{2,1,0:T(8,128)S(1)} %copy-done.2, ...), custom_call_target="tpu_custom_call" | custom-call | tf_op jit(solution)/shard_map/relax/pallas_call | solution.py:510
Async XLA Ops:
  0.0 15.9 %copy-start = (f32[5,8,32,128]{3,2,1,0:T(8,128)S(1)}, f32[5,8,32,128]{3,2,1,0:T(8,128)}, u32[]{:S(2)}) copy-start(f32[5,8,32,128]{3,2,1,0:T(8,128)} %field_ref.5) | copy-start | bytes 1966084
  0.0 15.9 %copy-start.1 = (f32[3,8,32,128]{3,2,1,0:T(8,128)S(1)}, f32[3,8,32,128]{3,2,1,0:T(8,128)}, u32[]{:S(2)}) copy-start(f32[3,8,32,128]{3,2,1,0:T(8,128)} %jitter_ref.3) | copy-start | bytes 1179652
  1.1 14.7 %collective-permute-start = (f32[8,1,32,128]{3,2,1,0:T(8,128)S(1)}, f32[8,1,32,128]{3,2,1,0:T(8,128)S(1)}, u32[]{:S(2)}, u32[]{:S(2)}) collective-permute-start(f32[8,1,32,128]{3,2,1,0:T(8,128)S(1)} %get-tuple-element.10), channel_id=1, source_target_pairs={{0,3},{1,0},{2,1},{3,2},{4,7},{5,4},{6,5},{7,6},{8,11},{9,8},{10,9... | collective-permute-start | bytes 393224 | tf_op jit(solution)/shard_map/ppermute | solution.py:21
  3.5 12.3 %collective-permute-start.1 = (f32[5,1,32,128]{3,2,1,0:T(8,128)S(1)}, f32[5,1,32,128]{3,2,1,0:T(8,128)S(1)}, u32[]{:S(2)}, u32[]{:S(2)}) collective-permute-start(f32[5,1,32,128]{3,2,1,0:T(8,128)S(1)} %get-tuple-element.11), channel_id=1, source_target_pairs={{0,1},{1,2},{2,3},{3,0},{4,5},{5,6},{6,7},{7,4},{8,9},{9,10},{10,1... | collective-permute-start | bytes 245768 | tf_op jit(solution)/shard_map/ppermute | solution.py:21
  17.6 9.4 %copy-start.2 = (f32[8,32,128]{2,1,0:T(8,128)S(1)}, f32[8,32,128]{2,1,0:T(8,128)}, u32[]{:S(2)}) copy-start(f32[8,32,128]{2,1,0:T(8,128)} %ratio_ref.1) | copy-start | bytes 393220
